TPU v7x, 256 devices: a whole 4x4x8 slice. The times are simulated.
256 devices in a mesh: rep: 16 (over y_hi, x, core), fsdp: 16 (over z, y_lo).
Axes of the slice: x: 4, y: 4 (y_hi: 2, y_lo: 2; y = y_hi * 2 + y_lo), z: 8, core: 2. Of those that a mesh axis runs over, the one named last changes fastest.
Arguments:
- tokens: bfloat16 [16, 8192, 3584], P('rep', 'fsdp'), may hold values from -6 to 6
- gain: float32 [3584], replicated, may hold values from 0.1 to 1.9
- cotangent: bfloat16 [16, 8192, 1024], P('rep', 'fsdp'), may hold values from -6 to 6
- params: float32 [16, 3584, 1024], P('rep', 'fsdp'), may hold values from -6 to 6
- momentum: float32 [16, 3584, 1024], P('rep', 'fsdp'), may hold values from -6 to 6
- step: int32 [1], replicated, may hold values from 0 to 2999
Outputs:
- keys: bfloat16 [16, 8192, 1024], P('rep', 'fsdp')
- input_gradient: bfloat16 [16, 8192, 3584], P('rep', 'fsdp')
- averaged: float32 [16, 3584, 1024], P('rep', 'fsdp')
- new_momentum: float32 [16, 3584, 1024], P('rep', 'fsdp')
All inputs are finite; a program needn't handle non-finite values.
Results may differ from a plain program's by a relative error of at most 0.02.
Values may be sent and summed in bfloat16 or wider, within the bound.
No kernel may reach another device: no remote copies, remote signals or barrier semaphores. Data moves between devices by JAX's collectives and lax.ppermute only.
A program may use at most 128 MiB of HBM per device.

v0:
```python
from functools import partial

import jax
import jax.numpy as jnp
from jax import lax
from jax.experimental import pallas as pl
from jax.experimental.pallas import tpu as pltpu
from jax.sharding import Mesh, PartitionSpec as P

BETA = 0.9
LRATE = 0.1
EPS = 1e-06
ROWS = ("z", "y")
FIRST = ((4, 1), (3, 1), (-3, 1), (4, 0))
SECOND = ((2, 1), (-2, 1), (1, 1), (-1, 1), (0, 1))
SECOND += ((3, 0), (-3, 0), (2, 0), (-2, 0), (1, 0), (-1, 0), (0, 0))


def ring(n, by):
    return [(i, (i + by) % n) for i in range(n)]


def up(value):
    return lax.ppermute(value, "z", ring(lax.axis_size("z"), 1))


def down(value):
    return lax.ppermute(value, "z", ring(lax.axis_size("z"), -1))


def across(value):
    return lax.ppermute(value, "y", [(0, 1), (1, 0)])


def swapped(value, bit):
    mask = 2**bit
    pairs = [(source, source ^ mask) for source in range(lax.axis_size("rep"))]
    return lax.ppermute(value, "rep", pairs)


def after(value, *others):
    return lax.optimization_barrier((value,) + others)[0]


def wide(value):
    return value.astype(jnp.float32)


def narrow(value):
    return value.astype(jnp.bfloat16)


def shard_at(by, column):
    z, y = lax.axis_index("z"), lax.axis_index("y")
    return 2 * lax.rem(z + (by + 8), 8) + lax.rem(y + column, 2)


def call(kernel, inputs, out_shape, scratch=(), anywhere=0, mib=16, flops=0, moved=0):
    vmem = pl.BlockSpec(memory_space=pltpu.VMEM)
    free = pl.BlockSpec(memory_space=pl.ANY)
    return pl.pallas_call(
        kernel,
        in_specs=[vmem] * (len(inputs) - anywhere) + [free] * anywhere,
        out_specs=[vmem] * len(out_shape),
        out_shape=[jax.ShapeDtypeStruct(shape, dtype) for shape, dtype in out_shape],
        scratch_shapes=list(scratch),
        compiler_params=pltpu.CompilerParams(vmem_limit_bytes=mib * 2**20),
        cost_estimate=pl.CostEstimate(flops=flops, bytes_accessed=moved, transcendentals=0),
    )(*inputs)


def cast_kernel(params, out):
    out[...] = params[...].astype(out.dtype)


def gain_row(gain):
    return jnp.concatenate([gain[i : i + 1, :] for i in range(gain.shape[0])], axis=1)


def grad_part(block, cot, out, at):
    part, features = block.shape[1], cot.shape[1]
    scale = (16 * part) ** (-0.5)
    for col in range(0, features, 256):
        product = lax.dot_general(
            block,
            cot[:, col : col + 256],
            (((0,), (0,)), ((), ())),
            preferred_element_type=jnp.float32,
        )
        out[at : at + part, col : col + 256] = (product * scale).astype(out.dtype)


def first_kernel(tokens, gain, cot, blocks, inverse, far, third, far_own):
    count, rows, part = blocks.shape
    width = tokens.shape[1]
    chunk = 64
    gains = gain_row(gain)

    @pl.loop(0, rows // chunk)
    def _(i):
        here = pl.ds(pl.multiple_of(i * chunk, chunk), chunk)
        x = tokens[here, :].astype(jnp.float32)
        inv = lax.rsqrt(jnp.sum(x * x, axis=1, keepdims=True) * (1.0 / width) + EPS)
        inverse[here, :] = inv
        normalized = ((x * inv) * gains).astype(jnp.bfloat16)
        for j in range(count):
            blocks[j, here, :] = normalized[:, j * part : (j + 1) * part]

    places = ((far, 0), (third, 0), (third, part), (far_own, 0))
    for (by, column), (out, at) in zip(FIRST, places):
        grad_part(blocks[shard_at(by, column)], cot, out, at)


def second_kernel(blocks, cot, *outs):
    part = blocks.shape[2]
    places = [(out, at) for out in outs for at in range(0, out.shape[0], part)]
    for (by, column), (out, at) in zip(SECOND, places):
        grad_part(blocks[shard_at(by, column)], cot, out, at)


def pieces(part):
    half = part // 2
    return (
        (0, 0, part, 0, 0, 0),
        (1, 0, part, 0, 1, 0),
        (2, 0, part, -1, 0, 0),
        (3, 0, part, 1, 0, 0),
        (4, 0, part, -2, 0, 0),
        (4, part, part, -1, 1, 0),
        (5, 0, part, 1, 1, 0),
        (5, part, part, 2, 0, 0),
        (6, 0, part, -3, 0, 0),
        (6, part, part, -2, 1, 0),
        (7, 0, part, 2, 1, 0),
        (7, part, part, 3, 0, 0),
        (8, 0, half, 4, 0, half),
        (8, half, part, -3, 1, 0),
        (9, 0, part, 3, 1, 0),
        (9, part, half, 4, 0, 0),
        (10, 0, part, 4, 1, 0),
    )


def lay_out(gathered, whole):
    part = whole.shape[0] // 16
    for array, at, count, by, column, inner in pieces(part):
        to = pl.multiple_of(shard_at(by, column) * part + inner, 16)
        whole[pl.ds(to, count), :] = gathered[array][at : at + count, :]


def add_products(blocks, shards, first, out, scale):
    part = blocks.shape[2]
    for col in range(0, out.shape[1], 256):
        total = None if first is None else first[:, col : col + 256]
        for number, rows, at in shards:
            product = jnp.dot(
                blocks[number],
                rows[at : at + part, col : col + 256],
                preferred_element_type=jnp.float32,
            )
            total = product if total is None else total + product
        out[:, col : col + 256] = (total * scale).astype(out.dtype)


def near_keys_kernel(blocks, *refs):
    gathered, out = refs[:8], refs[8]
    wanted = [piece for piece in pieces(blocks.shape[2]) if piece[0] < 8]
    shards = [(shard_at(by, column), gathered[i], at) for i, at, _, by, column, _ in wanted]
    add_products(blocks, shards, None, out, 1.0)


def far_keys_kernel(blocks, near, up4, down4, far, far_other, out):
    part = blocks.shape[2]
    shards = [
        (shard_at(-3, 1), up4, part // 2),
        (shard_at(3, 1), down4, 0),
        (shard_at(4, 0), far, 0),
        (shard_at(4, 1), far_other, 0),
    ]
    add_products(blocks, shards, near, out, (16 * part) ** (-0.5))


def input_kernel(gain, inverse, cot, tokens, *refs):
    gathered, (out, whole) = refs[:11], refs[11:]
    rows, width = tokens.shape
    lay_out(gathered, whole)
    gains = gain_row(gain) * width ** (-0.5)
    inv = inverse[...]
    total = jnp.zeros((rows, 1), jnp.float32)
    cols = 256
    for col in range(0, width, cols):
        product = lax.dot_general(
            cot[...],
            whole[col : col + cols, :],
            (((1,), (1,)), ((), ())),
            preferred_element_type=jnp.float32,
        )
        value = product * gains[:, col : col + cols]
        out[:, col : col + cols] = value.astype(out.dtype)
        total += jnp.sum(
            value * tokens[:, col : col + cols].astype(jnp.float32), axis=1, keepdims=True
        )
    token_scale = total * inv * inv * inv * (1.0 / width)
    chunk = 64
    for at in range(0, rows, chunk):
        here = slice(at, at + chunk)
        x = tokens[here, :].astype(jnp.float32)
        upstream = out[here, :].astype(jnp.float32)
        out[here, :] = (upstream * inv[here] - x * token_scale[here]).astype(out.dtype)


def update_kernel(own, first, rising, falling, params, momentum, new_momentum, updated, sent):
    part = own.shape[0]
    grad = own[...].astype(jnp.float32) + first[2 * part :, :].astype(jnp.float32)
    grad += rising[...].astype(jnp.float32) + falling[...].astype(jnp.float32)
    moved = BETA * momentum[...] + grad
    new_momentum[...] = moved
    value = params[...] - LRATE * moved
    updated[...] = value
    sent[...] = value.astype(sent.dtype)


def average_kernel(updated, peer, out):
    out[...] = 0.5 * (updated[...] + peer[...].astype(jnp.float32))


def local(tokens, gain, cotangent, params, momentum, step):
    rows, width = tokens.shape[1:]
    features = cotangent.shape[2]
    part, half = params.shape[1], params.shape[1] // 2
    which = jnp.remainder(step[0], 3)
    param_rows, tokens, cot = params[0], tokens[0], cotangent[0]
    gain = gain.reshape(width // 128, 128)
    bf16, f32 = jnp.bfloat16, jnp.float32

    def sums(*counts):
        return [((n * part, features), bf16) for n in counts]

    product = 2 * rows * part * features
    (own,) = call(cast_kernel, [param_rows], sums(1), moved=2**20)
    up1, down1, other = up(own), down(own), across(own)
    blocks, inverse, far, third, far_own = call(
        first_kernel,
        [tokens, gain, cot],
        [((16, rows, part), bf16), ((rows, 1), f32)] + sums(1, 2, 1),
        flops=4 * product,
        moved=11 * 2**20,
    )
    up2, down2 = jnp.concatenate([up1, other]), jnp.concatenate([other, down1])
    far = across(far)
    up2, down2, third = lax.optimization_barrier((up2, down2, third))
    up2, down2, third = up(up2), down(down2), across(third)
    sent = narrow(wide(far_own) + wide(far))
    sent, blocks = lax.optimization_barrier((sent, blocks))
    rising, falling = up(sent[:half]), down(sent[half:])
    second, first, own3, own2, own1, own0 = call(
        second_kernel,
        [blocks, cot],
        sums(2, 3, 2, 2, 2, 1),
        flops=12 * product,
        moved=11 * 2**20,
    )

    def reduced(owns, received, rising, falling, *earlier):
        plus = wide(owns[:part]) + wide(received[:part]) + wide(rising)
        minus = wide(owns[part:]) + wide(received[part : 2 * part]) + wide(falling)
        return lax.optimization_barrier((narrow(plus), narrow(minus)) + earlier)[:2]

    up2, down2, rising, falling, second = lax.optimization_barrier(
        (up2, down2, rising, falling, second)
    )
    up3, down3 = up(up2), down(down2)
    second = across(after(second, up2, down2))
    empty = jnp.zeros((half, features), bf16)
    rising, falling = jnp.concatenate([rising, empty]), jnp.concatenate([empty, falling])
    plus, minus = reduced(own3, third, rising, falling, up2, down2)
    rising, falling = up(plus), down(minus)

    up4, down4 = up(up3[half:]), down(down3[: part + half])
    first = across(after(first, up3, down3))
    plus, minus = reduced(own2, second, rising, falling, up3, down3)
    rising, falling = up(plus), down(minus)
    blocks = after(blocks, plus, minus)
    (near,) = call(
        near_keys_kernel,
        [blocks, own, other, up1, down1, up2, down2, up3, down3],
        [((rows, features), f32)],
        flops=12 * product,
        moved=12 * 2**20,
    )
    far_rows = after(jnp.concatenate([down4[part:], up4[:half]]), near)
    far_other = across(far_rows)
    plus, minus = reduced(own1, first, rising, falling, up4, down4)
    rising, falling = up(plus), down(minus)

    (keys,) = call(
        far_keys_kernel,
        [after(blocks, plus, minus), near, up4, down4, far_rows, far_other],
        [((rows, features), bf16)],
        flops=4 * product,
        moved=9 * 2**20,
    )
    gathered = [own, other, up1, down1, up2, down2, up3, down3, up4, down4, far_other]
    (input_gradient,) = call(
        input_kernel,
        [gain, inverse, cot, after(tokens, plus, minus)] + gathered,
        [((rows, width), bf16)],
        [pltpu.VMEM((width, features), bf16)],
        mib=26,
        flops=16 * product,
        moved=16 * 2**20,
    )
    stored = ((part, features), f32)
    new_momentum, updated, sent = call(
        update_kernel,
        [own0, first, rising, falling, param_rows, momentum[0]],
        [stored, stored] + sums(1),
        moved=6 * 2**20,
    )

    peer = lax.switch(
        which, [partial(swapped, bit=b) for b in range(3)], after(sent, keys, input_gradient)
    )
    (averaged,) = call(average_kernel, [updated, peer], [stored], moved=2 * 2**20)
    return (keys[None], input_gradient[None], averaged[None], new_momentum[None])


def solution(mesh):
    split = Mesh(mesh.devices.reshape(mesh.devices.shape[0], -1, 2), ("rep",) + ROWS)
    rows = P("rep", ROWS, None)
    return jax.shard_map(
        local,
        mesh=split,
        in_specs=(rows, P(), rows, rows, rows, P()),
        out_specs=(rows,) * 4,
        check_vma=False,
    )
```

profile of v0, /device:TPU:8, one launch (start us, length us, event | category | flops | bytes accessed | tf_op | source)
XLA Modules:
  0.0 146.6 jit_solution(14212593676575018333)
XLA Ops:
  2.0 5.9 %collective-permute-start.6 = (bf16[224,1024]{1,0:T(8,128)(2,1)S(1)}, bf16[224,1024]{1,0:T(8,128)(2,1)S(1)}, u32[]{:S(2)}, u32[]{:S(2)}) collective-permute-start(bf16[224,1024]{1,0:T(8,128)(2,1)S(1)} %shard_map.95.refs_0_), channel_id=1, source_target_pairs={{0,14},{2,0},{4,2},{6,4},{8,6},{10,8},{12,10},{14,12},{1,15},{3,1}... | collective-permute-start | bytes 1376264 | tf_op jit(solution)/shard_map/ppermute | solution.py:28
  11.1 4.5 %shard_map.93 = (bf16[16,512,224]{2,1,0:T(8,128)(2,1)S(1)}, f32[512,1]{1,0:T(8,128)S(1)}, bf16[224,1024]{1,0:T(8,128)(2,1)S(1)}, bf16[448,1024]{1,0:T(8,128)(2,1)S(1)}, bf16[224,1024]{1,0:T(8,128)(2,1)S(1)}) custom-call(bf16[512,3584]{1,0:T(8,128)(2,1)S(1)} %bitcast.10, f32[28,128]{1,0:T(8,128)S(1)} %bitcast.18, bf16[512,1024]{1,0:T(8,128)(2,1)S(1)} %bitcast.12), custom_call_target="tpu_custom_call" | custom-call | flops 939524096 | bytes 11534336 | tf_op jit(solution)/shard_map/pallas_call | solution.py:61
  17.7 3.7 %collective-permute-done.5.refs_1_ = bf16[224,1024]{1,0:T(8,128)(2,1)S(1)} collective-permute-done((bf16[224,1024]{1,0:T(8,128)(2,1)S(1)}, bf16[224,1024]{1,0:T(8,128)(2,1)S(1)}, u32[]{:S(2)}, u32[]{:S(2)}) %collective-permute-start.5) | collective-permute-done | bytes 458784 | tf_op jit(solution)/shard_map/ppermute | solution.py:32
  21.7 3.2 %collective-permute-start.8 = (bf16[448,1024]{1,0:T(8,128)(2,1)S(1)}, bf16[448,1024]{1,0:T(8,128)(2,1)S(1)}, u32[]{:S(2)}, u32[]{:S(2)}) collective-permute-start(bf16[448,1024]{1,0:T(8,128)(2,1)S(1)} %get-tuple-element.55), channel_id=1, source_target_pairs={{0,14},{2,0},{4,2},{6,4},{8,6},{10,8},{12,10},{14,12},{1,15},{3,1}... | collective-permute-start | bytes 2752520 | tf_op jit(solution)/shard_map/ppermute | solution.py:28
  24.9 4.8 %collective-permute-done.3 = bf16[224,1024]{1,0:T(8,128)(2,1)S(1)} collective-permute-done((bf16[224,1024]{1,0:T(8,128)(2,1)S(1)}, bf16[224,1024]{1,0:T(8,128)(2,1)S(1)}, u32[]{:S(2)}, u32[]{:S(2)}) %collective-permute-start.3) | collective-permute-done | bytes 458784 | tf_op jit(solution)/shard_map/ppermute | solution.py:32
  32.6 3.1 %shard_map.94 = (bf16[448,1024]{1,0:T(8,128)(2,1)S(1)}, bf16[672,1024]{1,0:T(8,128)(2,1)S(1)}, bf16[448,1024]{1,0:T(8,128)(2,1)S(1)}, bf16[448,1024]{1,0:T(8,128...) custom-call(bf16[16,512,224]{2,1,0:T(8,128)(2,1)S(1)} %get-tuple-element.76.blocks, ...), custom_call_target="tpu_custom_call" | custom-call | flops 2818572288 | bytes 11534336 | tf_op jit(solution)/shard_map/pallas_call | solution.py:61
  36.5 11.1 %collective-permute-done.10 = bf16[112,1024]{1,0:T(8,128)(2,1)S(1)} collective-permute-done((bf16[112,1024]{1,0:T(8,128)(2,1)S(1)}, bf16[112,1024]{1,0:T(8,128)(2,1)S(1)}, u32[]{:S(2)}, u32[]{:S(2)}) %collective-permute-start.10) | collective-permute-done | bytes 229408 | tf_op jit(solution)/shard_map/ppermute | solution.py:28
  48.4 3.2 %collective-permute-start.16 = (bf16[448,1024]{1,0:T(8,128)(2,1)S(1)}, bf16[448,1024]{1,0:T(8,128)(2,1)S(1)}, u32[]{:S(2)}, u32[]{:S(2)}) collective-permute-start(bf16[448,1024]{1,0:T(8,128)(2,1)S(1)} %collective-permute-done.8.refs_5_), channel_id=1, source_target_pairs={{0,14},{2,0},{4,2},{6,4},{8,6},{10,8},{12,10},{14,12},{1,15},{3,1}... | collective-permute-start | bytes 2752520 | tf_op jit(solution)/shard_map/ppermute | solution.py:28
  53.8 19.2 %collective-permute-done.15.refs_6_ = bf16[448,1024]{1,0:T(8,128)(2,1)S(1)} collective-permute-done((bf16[448,1024]{1,0:T(8,128)(2,1)S(1)}, bf16[448,1024]{1,0:T(8,128)(2,1)S(1)}, u32[]{:S(2)}, u32[]{:S(2)}) %collective-permute-start.15) | collective-permute-done | bytes 917536 | tf_op jit(solution)/shard_map/ppermute | solution.py:24
  76.7 6.0 %collective-permute-done.13 = bf16[224,1024]{1,0:T(8,128)(2,1)S(1)} collective-permute-done((bf16[224,1024]{1,0:T(8,128)(2,1)S(1)}, bf16[224,1024]{1,0:T(8,128)(2,1)S(1)}, u32[]{:S(2)}, u32[]{:S(2)}) %collective-permute-start.13) | collective-permute-done | bytes 458784 | tf_op jit(solution)/shard_map/ppermute | solution.py:24
  84.5 3.4 %collective-permute-done.14 = bf16[224,1024]{1,0:T(8,128)(2,1)S(1)} collective-permute-done((bf16[224,1024]{1,0:T(8,128)(2,1)S(1)}, bf16[224,1024]{1,0:T(8,128)(2,1)S(1)}, u32[]{:S(2)}, u32[]{:S(2)}) %collective-permute-start.14) | collective-permute-done | bytes 458784 | tf_op jit(solution)/shard_map/ppermute | solution.py:28
  88.5 3.2 %collective-permute-start.19 = (bf16[224,1024]{1,0:T(8,128)(2,1)S(1)}, bf16[224,1024]{1,0:T(8,128)(2,1)S(1)}, u32[]{:S(2)}, u32[]{:S(2)}) collective-permute-start(bf16[224,1024]{1,0:T(8,128)(2,1)S(1)} %get-tuple-element.69), channel_id=1, source_target_pairs={{0,14},{2,0},{4,2},{6,4},{8,6},{10,8},{12,10},{14,12},{1,15},{3,1}... | collective-permute-start | bytes 1376264 | tf_op jit(solution)/shard_map/ppermute | solution.py:28
  91.8 3.4 %shard_map.96.near = f32[512,1024]{1,0:T(8,128)S(1)} custom-call(bf16[16,512,224]{2,1,0:T(8,128)(2,1)S(1)} %get-tuple-element.76.blocks, bf16[224,1024]{1,0:T(8,128)(2,1)S(1)} %shard_map.95.refs_0_, bf16[224,1024]{1,0:T(8,128)(2,1)S(1)} %collective-permute-done.5.refs_1_, bf16[224,1024]{1,0:T(8,128)(2,1)S(1)} %collective-permute-done.4.refs_2_, ...), custom_call_target="tpu_custom_call" | custom-call | flops 2818572288 | bytes 12582912 | tf_op jit(solution)/shard_map/pallas_call | solution.py:61
  95.2 2.3 %collective-permute-done.20.up4.refs_8_ = bf16[336,1024]{1,0:T(8,128)(2,1)S(1)} collective-permute-done((bf16[336,1024]{1,0:T(8,128)(2,1)S(1)}, bf16[336,1024]{1,0:T(8,128)(2,1)S(1)}, u32[]{:S(2)}, u32[]{:S(2)}) %collective-permute-start.20) | collective-permute-done | bytes 688160 | tf_op jit(solution)/shard_map/ppermute | solution.py:24
  97.5 5.1 %collective-permute-done.21.down4.refs_9_ = bf16[336,1024]{1,0:T(8,128)(2,1)S(1)} collective-permute-done((bf16[336,1024]{1,0:T(8,128)(2,1)S(1)}, bf16[336,1024]{1,0:T(8,128)(2,1)S(1)}, u32[]{:S(2)}, u32[]{:S(2)}) %collective-permute-start.21) | collective-permute-done | bytes 688160 | tf_op jit(solution)/shard_map/ppermute | solution.py:28
  103.6 4.0 %collective-permute-done.19 = bf16[224,1024]{1,0:T(8,128)(2,1)S(1)} collective-permute-done((bf16[224,1024]{1,0:T(8,128)(2,1)S(1)}, bf16[224,1024]{1,0:T(8,128)(2,1)S(1)}, u32[]{:S(2)}, u32[]{:S(2)}) %collective-permute-start.19) | collective-permute-done | bytes 458784 | tf_op jit(solution)/shard_map/ppermute | solution.py:28
  109.2 3.2 %collective-permute-start.24 = (bf16[224,1024]{1,0:T(8,128)(2,1)}, bf16[224,1024]{1,0:T(8,128)(2,1)}, u32[]{:S(2)}, u32[]{:S(2)}) collective-permute-start(bf16[224,1024]{1,0:T(8,128)(2,1)} %get-tuple-element.75), channel_id=1, source_target_pairs={{0,14},{2,0},{4,2},{6,4},{8,6},{10,8},{12,10},{14,12},{1,15},{3,1}... | collective-permute-start | bytes 1376264 | tf_op jit(solution)/shard_map/ppermute | solution.py:28
  113.1 2.2 %copy-done.1 = bf16[16,512,224]{2,1,0:T(8,128)(2,1)S(1)} copy-done((bf16[16,512,224]{2,1,0:T(8,128)(2,1)S(1)}, bf16[16,512,224]{2,1,0:T(8,128)(2,1)}, u32[]{:S(2)}) %copy-start.1) | copy-done | bytes 3670040
  117.6 3.5 %shard_map.97 = bf16[512,1024]{1,0:T(8,128)(2,1)} custom-call(bf16[16,512,224]{2,1,0:T(8,128)(2,1)S(1)} %copy-done.1, f32[512,1024]{1,0:T(8,128)S(1)} %shard_map.96.near, bf16[336,1024]{1,0:T(8,128)(2,1)S(1)} %copy-done.17, bf16[336,1024]{1,0:T(8,128)(2,1)S(1)} %copy-done.20, bf16[224,1024]{1,0:T(8,128)(2,1)} %pad_maximum_fusion.2.far, ...), custom_call_target="tpu_custom_call" | custom-call | flops 939524096 | bytes 9437184 | tf_op jit(solution)/shard_map/pallas_call | solution.py:61
  123.0 9.0 %shard_map.98 = bf16[512,3584]{1,0:T(8,128)(2,1)} custom-call(f32[28,128]{1,0:T(8,128)S(1)} %bitcast.19, f32[512,1]{1,0:T(8,128)S(1)} %copy-done.32, bf16[512,1024]{1,0:T(8,128)(2,1)S(1)} %bitcast.14, bf16[512,3584]{1,0:T(8,128)(2,1)S(1)} %bitcast.11, bf16[224,1024]{1,0:T(8,128)(2,1)S(1)} %copy-done.13, bf16[224,1024]{1,0:T(8,128)(2,1)S(1)} %copy-done.9, ...), custom_call_target="tpu_custom_call" | custom-call | flops 3758096384 | bytes 16777216 | tf_op jit(solution)/shard_map/pallas_call | solution.py:61
  132.1 2.4 %shard_map.99 = (f32[224,1024]{1,0:T(8,128)}, f32[224,1024]{1,0:T(8,128)S(1)}, bf16[224,1024]{1,0:T(8,128)(2,1)S(1)}) custom-call(bf16[224,1024]{1,0:T(8,128)(2,1)S(1)} %copy-done.30, bf16[672,1024]{1,0:T(8,128)(2,1)S(1)} %copy-done.15, bf16[224,1024]{1,0:T(8,128)(2,1)} %collective-permute-done.23.rising, bf16[224,1024]{1,0:T(8,128)(2,1)} %collective-permute-done.24.falling, ...), custom_call_target="tpu_custom_call" | custom-call | bytes 6291456 | tf_op jit(solution)/shard_map/pallas_call | solution.py:61
  134.5 10.1 %conditional.1 = (bf16[224,1024]{1,0:T(8,128)(2,1)}) conditional(s32[]{:T(128)} %clamp.3, bf16[224,1024]{1,0:T(8,128)(2,1)S(1)} %get-tuple-element.83, bf16[224,1024]{1,0:T(8,128)(2,1)S(1)} %get-tuple-element.83, bf16[224,1024]{1,0:T(8,128)(2,1)S(1)} %get-tuple-element.83), branch_computations={%region_0.1_spmd, %region_1.2_spmd, %region_2.3_spmd} | conditional | bytes 1835056 | solution.py:321
  134.5 3.0 %collective-permute-start.2 = (bf16[224,1024]{1,0:T(8,128)(2,1)S(1)}, bf16[224,1024]{1,0:T(8,128)(2,1)}, u32[]{:S(2)}, u32[]{:S(2)}) collective-permute-start(bf16[224,1024]{1,0:T(8,128)(2,1)S(1)} %param.2), channel_id=1, source_target_pairs={{0,64},{16,80},{32,96},{48,112},{64,0},{80,16},{96,32},{112,48},{1... | collective-permute-start | bytes 1376264 | tf_op jit(solution)/shard_map/cond/branch_2_fun/ppermute | solution.py:38
  137.5 7.1 %collective-permute-done.2 = bf16[224,1024]{1,0:T(8,128)(2,1)} collective-permute-done((bf16[224,1024]{1,0:T(8,128)(2,1)S(1)}, bf16[224,1024]{1,0:T(8,128)(2,1)}, u32[]{:S(2)}, u32[]{:S(2)}) %collective-permute-start.2) | collective-permute-done | bytes 458784 | tf_op jit(solution)/shard_map/cond/branch_2_fun/ppermute | solution.py:38
  (112 shorter events, 28.3 us)
Async XLA Ops:
  2.0 89.8 %copy-start.12 = (bf16[224,1024]{1,0:T(8,128)(2,1)}, bf16[224,1024]{1,0:T(8,128)(2,1)S(1)}, u32[]{:S(2)}) copy-start(bf16[224,1024]{1,0:T(8,128)(2,1)S(1)} %shard_map.95.refs_0_) | copy-start | bytes 1376260
  2.0 15.7 %collective-permute-start.6 = (bf16[224,1024]{1,0:T(8,128)(2,1)S(1)}, bf16[224,1024]{1,0:T(8,128)(2,1)S(1)}, u32[]{:S(2)}, u32[]{:S(2)}) collective-permute-start(bf16[224,1024]{1,0:T(8,128)(2,1)S(1)} %shard_map.95.refs_0_), channel_id=1, source_target_pairs={{0,14},{2,0},{4,2},{6,4},{8,6},{10,8},{12,10},{14,12},{1,15},{3,1}... | collective-permute-start | bytes 1376264 | tf_op jit(solution)/shard_map/ppermute | solution.py:28
  7.9 13.4 %collective-permute-start.5 = (bf16[224,1024]{1,0:T(8,128)(2,1)S(1)}, bf16[224,1024]{1,0:T(8,128)(2,1)S(1)}, u32[]{:S(2)}, u32[]{:S(2)}) collective-permute-start(bf16[224,1024]{1,0:T(8,128)(2,1)S(1)} %shard_map.95.refs_0_), channel_id=1, source_target_pairs={{0,1},{1,0},{2,3},{3,2},{4,5},{5,4},{6,7},{7,6},{8,9},{9,8},{10,11... | collective-permute-start | bytes 1376264 | tf_op jit(solution)/shard_map/ppermute | solution.py:32
  8.4 13.0 %collective-permute-start.4 = (bf16[224,1024]{1,0:T(8,128)(2,1)S(1)}, bf16[224,1024]{1,0:T(8,128)(2,1)S(1)}, u32[]{:S(2)}, u32[]{:S(2)}) collective-permute-start(bf16[224,1024]{1,0:T(8,128)(2,1)S(1)} %shard_map.95.refs_0_), channel_id=1, source_target_pairs={{0,2},{2,4},{4,6},{6,8},{8,10},{10,12},{12,14},{14,0},{1,3},{3,5},... | collective-permute-start | bytes 1376264 | tf_op jit(solution)/shard_map/ppermute | solution.py:24
  15.6 14.1 %collective-permute-start.3 = (bf16[224,1024]{1,0:T(8,128)(2,1)S(1)}, bf16[224,1024]{1,0:T(8,128)(2,1)S(1)}, u32[]{:S(2)}, u32[]{:S(2)}) collective-permute-start(bf16[224,1024]{1,0:T(8,128)(2,1)S(1)} %get-tuple-element.49), channel_id=1, source_target_pairs={{0,1},{1,0},{2,3},{3,2},{4,5},{5,4},{6,7},{7,6},{8,9},{9,8},{10,11... | collective-permute-start | bytes 1376264 | tf_op jit(solution)/shard_map/ppermute | solution.py:32
  21.6 26.7 %collective-permute-start.7 = (bf16[448,1024]{1,0:T(8,128)(2,1)S(1)}, bf16[448,1024]{1,0:T(8,128)(2,1)S(1)}, u32[]{:S(2)}, u32[]{:S(2)}) collective-permute-start(bf16[448,1024]{1,0:T(8,128)(2,1)S(1)} %get-tuple-element.54), channel_id=1, source_target_pairs={{0,2},{2,4},{4,6},{6,8},{8,10},{10,12},{12,14},{14,0},{1,3},{3,5},... | collective-permute-start | bytes 2752520 | tf_op jit(solution)/shard_map/ppermute | solution.py:24
  21.7 26.6 %collective-permute-start.8 = (bf16[448,1024]{1,0:T(8,128)(2,1)S(1)}, bf16[448,1024]{1,0:T(8,128)(2,1)S(1)}, u32[]{:S(2)}, u32[]{:S(2)}) collective-permute-start(bf16[448,1024]{1,0:T(8,128)(2,1)S(1)} %get-tuple-element.55), channel_id=1, source_target_pairs={{0,14},{2,0},{4,2},{6,4},{8,6},{10,8},{12,10},{14,12},{1,15},{3,1}... | collective-permute-start | bytes 2752520 | tf_op jit(solution)/shard_map/ppermute | solution.py:28
  29.9 23.3 %collective-permute-start.12 = (bf16[448,1024]{1,0:T(8,128)(2,1)S(1)}, bf16[448,1024]{1,0:T(8,128)(2,1)S(1)}, u32[]{:S(2)}, u32[]{:S(2)}) collective-permute-start(bf16[448,1024]{1,0:T(8,128)(2,1)S(1)} %get-tuple-element.63), channel_id=1, source_target_pairs={{0,1},{1,0},{2,3},{3,2},{4,5},{5,4},{6,7},{7,6},{8,9},{9,8},{10,11... | collective-permute-start | bytes 2752520 | tf_op jit(solution)/shard_map/ppermute | solution.py:32
  30.5 17.1 %collective-permute-start.10 = (bf16[112,1024]{1,0:T(8,128)(2,1)S(1)}, bf16[112,1024]{1,0:T(8,128)(2,1)S(1)}, u32[]{:S(2)}, u32[]{:S(2)}) collective-permute-start(bf16[112,1024]{1,0:T(8,128)(2,1)S(1)} %get-tuple-element.91), channel_id=1, source_target_pairs={{0,14},{2,0},{4,2},{6,4},{8,6},{10,8},{12,10},{14,12},{1,15},{3,1}... | collective-permute-start | bytes 688136 | tf_op jit(solution)/shard_map/ppermute | solution.py:28
  32.3 16.0 %collective-permute-start.9 = (bf16[112,1024]{1,0:T(8,128)(2,1)S(1)}, bf16[112,1024]{1,0:T(8,128)(2,1)S(1)}, u32[]{:S(2)}, u32[]{:S(2)}) collective-permute-start(bf16[112,1024]{1,0:T(8,128)(2,1)S(1)} %get-tuple-element.92), channel_id=1, source_target_pairs={{0,2},{2,4},{4,6},{6,8},{8,10},{10,12},{12,14},{14,0},{1,3},{3,5},... | collective-permute-start | bytes 688136 | tf_op jit(solution)/shard_map/ppermute | solution.py:24
  48.3 24.6 %collective-permute-start.15 = (bf16[448,1024]{1,0:T(8,128)(2,1)S(1)}, bf16[448,1024]{1,0:T(8,128)(2,1)S(1)}, u32[]{:S(2)}, u32[]{:S(2)}) collective-permute-start(bf16[448,1024]{1,0:T(8,128)(2,1)S(1)} %collective-permute-done.7.refs_4_), channel_id=1, source_target_pairs={{0,2},{2,4},{4,6},{6,8},{8,10},{10,12},{12,14},{14,0},{1,3},{3,5},... | collective-permute-start | bytes 2752520 | tf_op jit(solution)/shard_map/ppermute | solution.py:24
  48.4 24.5 %collective-permute-start.16 = (bf16[448,1024]{1,0:T(8,128)(2,1)S(1)}, bf16[448,1024]{1,0:T(8,128)(2,1)S(1)}, u32[]{:S(2)}, u32[]{:S(2)}) collective-permute-start(bf16[448,1024]{1,0:T(8,128)(2,1)S(1)} %collective-permute-done.8.refs_5_), channel_id=1, source_target_pairs={{0,14},{2,0},{4,2},{6,4},{8,6},{10,8},{12,10},{14,12},{1,15},{3,1}... | collective-permute-start | bytes 2752520 | tf_op jit(solution)/shard_map/ppermute | solution.py:28
  51.7 36.2 %collective-permute-start.11 = (bf16[448,1024]{1,0:T(8,128)(2,1)S(1)}, bf16[448,1024]{1,0:T(8,128)(2,1)S(1)}, u32[]{:S(2)}, u32[]{:S(2)}) collective-permute-start(bf16[448,1024]{1,0:T(8,128)(2,1)S(1)} %get-tuple-element.61), channel_id=1, source_target_pairs={{0,1},{1,0},{2,3},{3,2},{4,5},{5,4},{6,7},{7,6},{8,9},{9,8},{10,11... | collective-permute-start | bytes 2752520 | tf_op jit(solution)/shard_map/ppermute | solution.py:32
  53.7 29.1 %collective-permute-start.13 = (bf16[224,1024]{1,0:T(8,128)(2,1)S(1)}, bf16[224,1024]{1,0:T(8,128)(2,1)S(1)}, u32[]{:S(2)}, u32[]{:S(2)}) collective-permute-start(bf16[224,1024]{1,0:T(8,128)(2,1)S(1)} %get-tuple-element.66), channel_id=1, source_target_pairs={{0,2},{2,4},{4,6},{6,8},{8,10},{10,12},{12,14},{14,0},{1,3},{3,5},... | collective-permute-start | bytes 1376264 | tf_op jit(solution)/shard_map/ppermute | solution.py:24
  72.9 34.7 %collective-permute-start.17 = (bf16[672,1024]{1,0:T(8,128)(2,1)S(1)}, bf16[672,1024]{1,0:T(8,128)(2,1)S(1)}, u32[]{:S(2)}, u32[]{:S(2)}) collective-permute-start(bf16[672,1024]{1,0:T(8,128)(2,1)S(1)} %get-tuple-element.73), channel_id=1, source_target_pairs={{0,1},{1,0},{2,3},{3,2},{4,5},{5,4},{6,7},{7,6},{8,9},{9,8},{10,11... | collective-permute-start | bytes 4128776 | tf_op jit(solution)/shard_map/ppermute | solution.py:32
  74.5 13.4 %collective-permute-start.14 = (bf16[224,1024]{1,0:T(8,128)(2,1)S(1)}, bf16[224,1024]{1,0:T(8,128)(2,1)S(1)}, u32[]{:S(2)}, u32[]{:S(2)}) collective-permute-start(bf16[224,1024]{1,0:T(8,128)(2,1)S(1)} %get-tuple-element.67), channel_id=1, source_target_pairs={{0,14},{2,0},{4,2},{6,4},{8,6},{10,8},{12,10},{14,12},{1,15},{3,1}... | collective-permute-start | bytes 1376264 | tf_op jit(solution)/shard_map/ppermute | solution.py:28
  76.3 21.2 %collective-permute-start.20 = (bf16[336,1024]{1,0:T(8,128)(2,1)S(1)}, bf16[336,1024]{1,0:T(8,128)(2,1)S(1)}, u32[]{:S(2)}, u32[]{:S(2)}) collective-permute-start(bf16[336,1024]{1,0:T(8,128)(2,1)S(1)} %slice.78), channel_id=1, source_target_pairs={{0,2},{2,4},{4,6},{6,8},{8,10},{10,12},{12,14},{14,0},{1,3},{3,5},... | collective-permute-start | bytes 2064392 | tf_op jit(solution)/shard_map/ppermute | solution.py:24
  82.7 19.9 %collective-permute-start.21 = (bf16[336,1024]{1,0:T(8,128)(2,1)S(1)}, bf16[336,1024]{1,0:T(8,128)(2,1)S(1)}, u32[]{:S(2)}, u32[]{:S(2)}) collective-permute-start(bf16[336,1024]{1,0:T(8,128)(2,1)S(1)} %slice.79), channel_id=1, source_target_pairs={{0,14},{2,0},{4,2},{6,4},{8,6},{10,8},{12,10},{14,12},{1,15},{3,1}... | collective-permute-start | bytes 2064392 | tf_op jit(solution)/shard_map/ppermute | solution.py:28
  88.4 15.2 %collective-permute-start.18 = (bf16[224,1024]{1,0:T(8,128)(2,1)S(1)}, bf16[224,1024]{1,0:T(8,128)(2,1)S(1)}, u32[]{:S(2)}, u32[]{:S(2)}) collective-permute-start(bf16[224,1024]{1,0:T(8,128)(2,1)S(1)} %get-tuple-element.68), channel_id=1, source_target_pairs={{0,2},{2,4},{4,6},{6,8},{8,10},{10,12},{12,14},{14,0},{1,3},{3,5},... | collective-permute-start | bytes 1376264 | tf_op jit(solution)/shard_map/ppermute | solution.py:24
  88.5 19.1 %collective-permute-start.19 = (bf16[224,1024]{1,0:T(8,128)(2,1)S(1)}, bf16[224,1024]{1,0:T(8,128)(2,1)S(1)}, u32[]{:S(2)}, u32[]{:S(2)}) collective-permute-start(bf16[224,1024]{1,0:T(8,128)(2,1)S(1)} %get-tuple-element.69), channel_id=1, source_target_pairs={{0,14},{2,0},{4,2},{6,4},{8,6},{10,8},{12,10},{14,12},{1,15},{3,1}... | collective-permute-start | bytes 1376264 | tf_op jit(solution)/shard_map/ppermute | solution.py:28
  103.5 9.6 %collective-permute-start.22 = (bf16[224,1024]{1,0:T(8,128)(2,1)}, bf16[224,1024]{1,0:T(8,128)(2,1)}, u32[]{:S(2)}, u32[]{:S(2)}) collective-permute-start(bf16[224,1024]{1,0:T(8,128)(2,1)} %pad_maximum_fusion.2.far), channel_id=1, source_target_pairs={{0,1},{1,0},{2,3},{3,2},{4,5},{5,4},{6,7},{7,6},{8,9},{9,8},{10,11... | collective-permute-start | bytes 1376264 | tf_op jit(solution)/shard_map/ppermute | solution.py:32
  109.1 23.0 %collective-permute-start.23 = (bf16[224,1024]{1,0:T(8,128)(2,1)}, bf16[224,1024]{1,0:T(8,128)(2,1)}, u32[]{:S(2)}, u32[]{:S(2)}) collective-permute-start(bf16[224,1024]{1,0:T(8,128)(2,1)} %get-tuple-element.74), channel_id=1, source_target_pairs={{0,2},{2,4},{4,6},{6,8},{8,10},{10,12},{12,14},{14,0},{1,3},{3,5},... | collective-permute-start | bytes 1376264 | tf_op jit(solution)/shard_map/ppermute | solution.py:24
  109.2 22.9 %collective-permute-start.24 = (bf16[224,1024]{1,0:T(8,128)(2,1)}, bf16[224,1024]{1,0:T(8,128)(2,1)}, u32[]{:S(2)}, u32[]{:S(2)}) collective-permute-start(bf16[224,1024]{1,0:T(8,128)(2,1)} %get-tuple-element.75), channel_id=1, source_target_pairs={{0,14},{2,0},{4,2},{6,4},{8,6},{10,8},{12,10},{14,12},{1,15},{3,1}... | collective-permute-start | bytes 1376264 | tf_op jit(solution)/shard_map/ppermute | solution.py:28
  134.5 10.1 %collective-permute-start.2 = (bf16[224,1024]{1,0:T(8,128)(2,1)S(1)}, bf16[224,1024]{1,0:T(8,128)(2,1)}, u32[]{:S(2)}, u32[]{:S(2)}) collective-permute-start(bf16[224,1024]{1,0:T(8,128)(2,1)S(1)} %param.2), channel_id=1, source_target_pairs={{0,64},{16,80},{32,96},{48,112},{64,0},{80,16},{96,32},{112,48},{1... | collective-permute-start | bytes 1376264 | tf_op jit(solution)/shard_map/cond/branch_2_fun/ppermute | solution.py:38
  (34 other events, 452.8 us)
where the time goes:
time: 146 us; the launch traced here: 147 us
  waiting for transfers between devices  67.8 us (46%)
  starting transfers between devices  34.1 us (23%)
  Pallas kernels  28 us (19%)
  local copies, waits for them, and re-layouts  11.3 us (8%)
  other arithmetic  3.63 us (2%)
  between operations  1.68 us (1%)
    ppermute x8, waiting for transfers between devices, up(): return lax.ppermute(value, 'z', ring(lax.axis_size('z'), 1))  28.3 us
    pallas_call x8, Pallas kernels, call(): pl.pallas_call(kernel, in_specs=[vmem] * (len(inputs) - anywhere) + [free...  28 us
    ppermute x8, starting transfers between devices, down(): return lax.ppermute(value, 'z', ring(lax.axis_size('z'), -1))  24.2 us
    ppermute x8, waiting for transfers between devices, down(): return lax.ppermute(value, 'z', ring(lax.axis_size('z'), -1))  24 us
    unnamed x70, local copies, waits for them, and re-layouts  11.2 us
    ppermute x6, waiting for transfers between devices, across(): return lax.ppermute(value, 'y', [(0, 1), (1, 0)])  8.48 us
    ppermute x1, waiting for transfers between devices, swapped(): return lax.ppermute(value, 'rep', pairs)  7.06 us
    ppermute x6, starting transfers between devices, across(): return lax.ppermute(value, 'y', [(0, 1), (1, 0)])  5.86 us
  transfers between devices with their start and end apart: 23, of which 13 were waited for; matrix products, arithmetic and copies ran while one was open for 3% of the time, Pallas kernels for 16%

commit v1 on v0

--- a/solution.py
+++ b/solution.py
@@ -141,53 +141,56 @@
     )
 
 
-def lay_out(gathered, whole):
-    part = whole.shape[0] // 16
-    for array, at, count, by, column, inner in pieces(part):
-        to = pl.multiple_of(shard_at(by, column) * part + inner, 16)
-        whole[pl.ds(to, count), :] = gathered[array][at : at + count, :]
-
-
-def add_products(blocks, shards, first, out, scale):
+def near_keys_kernel(blocks, *refs):
+    gathered, out = refs[:8], refs[8]
     part = blocks.shape[2]
+    wanted = [piece for piece in pieces(part) if piece[0] < 8]
     for col in range(0, out.shape[1], 256):
-        total = None if first is None else first[:, col : col + 256]
-        for number, rows, at in shards:
+        total = None
+        for array, at, _, by, column, _ in wanted:
             product = jnp.dot(
-                blocks[number],
-                rows[at : at + part, col : col + 256],
+                blocks[shard_at(by, column)],
+                gathered[array][at : at + part, col : col + 256],
                 preferred_element_type=jnp.float32,
             )
             total = product if total is None else total + product
-        out[:, col : col + 256] = (total * scale).astype(out.dtype)
-
-
-def near_keys_kernel(blocks, *refs):
-    gathered, out = refs[:8], refs[8]
-    wanted = [piece for piece in pieces(blocks.shape[2]) if piece[0] < 8]
-    shards = [(shard_at(by, column), gathered[i], at) for i, at, _, by, column, _ in wanted]
-    add_products(blocks, shards, None, out, 1.0)
-
-
-def far_keys_kernel(blocks, near, up4, down4, far, far_other, out):
-    part = blocks.shape[2]
-    shards = [
-        (shard_at(-3, 1), up4, part // 2),
-        (shard_at(3, 1), down4, 0),
-        (shard_at(4, 0), far, 0),
-        (shard_at(4, 1), far_other, 0),
-    ]
-    add_products(blocks, shards, near, out, (16 * part) ** (-0.5))
-
-
-def input_kernel(gain, inverse, cot, tokens, *refs):
-    gathered, (out, whole) = refs[:11], refs[11:]
+        out[:, col : col + 256] = total
+
+
+def last_kernel(gain, inverse, *refs):
+    (tokens_far, cot_far, blocks_far, near_far), gathered = refs[:4], refs[4:15]
+    keys, out, whole, tokens, cot, blocks, near, sems = refs[15:]
     rows, width = tokens.shape
-    lay_out(gathered, whole)
+    part = width // 16
+    shards = [shard_at(by, column) for by, column in ((-3, 1), (3, 1), (4, 0), (4, 1))]
+    pairs = [(near_far, near)]
+    pairs += [(blocks_far.at[number], blocks.at[i]) for i, number in enumerate(shards)]
+    early = len(pairs) + 5
+    for array, at, count, by, column, inner in sorted(pieces(part), key=lambda p: p[0] < 8):
+        to = pl.multiple_of(shard_at(by, column) * part + inner, 16)
+        pairs.append((gathered[array].at[pl.ds(at, count), :], whole.at[pl.ds(to, count), :]))
+    pairs += [(cot_far, cot), (tokens_far, tokens)]
+    copies = [pltpu.make_async_copy(*pair, sems.at[i]) for i, pair in enumerate(pairs)]
+    for copy in copies:
+        copy.start()
     gains = gain_row(gain) * width ** (-0.5)
     inv = inverse[...]
+    for copy in copies[:early]:
+        copy.wait()
+    cols = 256
+    for col in range(0, keys.shape[1], cols):
+        total = near[:, col : col + cols]
+        for i, number in enumerate(shards):
+            at = pl.multiple_of(number * part, 16)
+            total += jnp.dot(
+                blocks[i],
+                whole[pl.ds(at, part), col : col + cols],
+                preferred_element_type=jnp.float32,
+            )
+        keys[:, col : col + cols] = (total * width ** (-0.5)).astype(keys.dtype)
+    for copy in copies[early:]:
+        copy.wait()
     total = jnp.zeros((rows, 1), jnp.float32)
-    cols = 256
     for col in range(0, width, cols):
         product = lax.dot_general(
             cot[...],
@@ -293,22 +296,23 @@
     plus, minus = reduced(own1, first, rising, falling, up4, down4)
     rising, falling = up(plus), down(minus)
 
-    (keys,) = call(
-        far_keys_kernel,
-        [after(blocks, plus, minus), near, up4, down4, far_rows, far_other],
-        [((rows, features), bf16)],
-        flops=4 * product,
-        moved=9 * 2**20,
-    )
     gathered = [own, other, up1, down1, up2, down2, up3, down3, up4, down4, far_other]
-    (input_gradient,) = call(
-        input_kernel,
-        [gain, inverse, cot, after(tokens, plus, minus)] + gathered,
-        [((rows, width), bf16)],
-        [pltpu.VMEM((width, features), bf16)],
-        mib=26,
-        flops=16 * product,
-        moved=16 * 2**20,
+    keys, input_gradient = call(
+        last_kernel,
+        [gain, inverse, tokens, cot, after(blocks, plus, minus), near] + gathered,
+        [((rows, features), bf16), ((rows, width), bf16)],
+        [
+            pltpu.VMEM((width, features), bf16),
+            pltpu.VMEM((rows, width), bf16),
+            pltpu.VMEM((rows, features), bf16),
+            pltpu.VMEM((4, rows, part), bf16),
+            pltpu.VMEM((rows, features), f32),
+            pltpu.SemaphoreType.DMA((24,)),
+        ],
+        15,
+        mib=34,
+        flops=20 * product,
+        moved=20 * 2**20,
     )
     stored = ((part, features), f32)
     new_momentum, updated, sent = call(

time: 146 us -> 149 us (1.021); the launches traced: 147 us -> 146 us
  waiting for transfers between devices: 67.8 us -> 58.7 us
  local copies, waits for them, and re-layouts: 11.3 us -> 19.4 us
  Pallas kernels: 28 us -> 29.9 us
  starting transfers between devices: 34.1 us -> 32.4 us
    unnamed x70 -> x66, local copies, waits for them, and re-layouts: 11.2 us -> 19.3 us
    ppermute x8, starting transfers between devices: 24.2 us -> 17.6 us  [down(): return lax.ppermute(value, 'z', ring(lax.axis_size('z'), -1))]
    ppermute x8, starting transfers between devices: 1.02 us -> 7.11 us  [up(): return lax.ppermute(value, 'z', ring(lax.axis_size('z'), 1))]
    ppermute x1, waiting for transfers between devices: 7.06 us -> 1.95 us  [swapped(): return lax.ppermute(value, 'rep', pairs)]
    ppermute x1, starting transfers between devices: 3.02 us -> 0.01 us  [swapped(): return lax.ppermute(value, 'rep', pairs)]
    ppermute x6, waiting for transfers between devices: 8.48 us -> 5.6 us  [across(): return lax.ppermute(value, 'y', [(0, 1), (1, 0)])]
    pallas_call x8 -> x7, Pallas kernels: 28 us -> 29.9 us  [call(): pl.pallas_call(kernel, in_specs=[vmem] * (len(inputs) - anywhere) + [free...]
    ppermute x6, starting transfers between devices: 5.86 us -> 7.7 us  [across(): return lax.ppermute(value, 'y', [(0, 1), (1, 0)])]
  transfers between devices with their start and end apart: 23 -> 23, of which waited for: 13 -> 11; matrix products, arithmetic and copies ran while one was open for 3% -> 3% of each run, Pallas kernels for 16% -> 17%
where the time goes in v1:
time: 149 us; the launch traced here: 146 us
  waiting for transfers between devices  58.7 us (39%)
  starting transfers between devices  32.4 us (22%)
  Pallas kernels  29.9 us (20%)
  local copies, waits for them, and re-layouts  19.4 us (13%)
  other arithmetic  3.74 us (3%)
  between operations  1.63 us (1%)
    pallas_call x7, Pallas kernels, call(): pl.pallas_call(kernel, in_specs=[vmem] * (len(inputs) - anywhere) + [free...  29.9 us
    ppermute x8, waiting for transfers between devices, up(): return lax.ppermute(value, 'z', ring(lax.axis_size('z'), 1))  27.2 us
    ppermute x8, waiting for transfers between devices, down(): return lax.ppermute(value, 'z', ring(lax.axis_size('z'), -1))  24 us
    unnamed x66, local copies, waits for them, and re-layouts  19.3 us
    ppermute x8, starting transfers between devices, down(): return lax.ppermute(value, 'z', ring(lax.axis_size('z'), -1))  17.6 us
    ppermute x6, starting transfers between devices, across(): return lax.ppermute(value, 'y', [(0, 1), (1, 0)])  7.7 us
    ppermute x8, starting transfers between devices, up(): return lax.ppermute(value, 'z', ring(lax.axis_size('z'), 1))  7.11 us
    ppermute x6, waiting for transfers between devices, across(): return lax.ppermute(value, 'y', [(0, 1), (1, 0)])  5.6 us
  transfers between devices with their start and end apart: 23, of which 11 were waited for; matrix products, arithmetic and copies ran while one was open for 3% of the time, Pallas kernels for 17%

profile of v1, /device:TPU:8, one launch (start us, length us, event | category | flops | bytes accessed | tf_op | source)
XLA Modules:
  0.0 145.7 jit_solution(8502302109199774061)
XLA Ops:
  2.0 2.0 %collective-permute-start.4 = (bf16[224,1024]{1,0:T(8,128)(2,1)S(1)}, bf16[224,1024]{1,0:T(8,128)(2,1)S(1)}, u32[]{:S(2)}, u32[]{:S(2)}) collective-permute-start(bf16[224,1024]{1,0:T(8,128)(2,1)S(1)} %shard_map.95.refs_0_.refs_4_), channel_id=1, source_target_pairs={{0,2},{2,4},{4,6},{6,8},{8,10},{10,12},{12,14},{14,0},{1,3},{3,5},... | collective-permute-start | bytes 1376264 | tf_op jit(solution)/shard_map/ppermute | solution.py:24
  4.4 4.0 %collective-permute-start.6 = (bf16[224,1024]{1,0:T(8,128)(2,1)S(1)}, bf16[224,1024]{1,0:T(8,128)(2,1)S(1)}, u32[]{:S(2)}, u32[]{:S(2)}) collective-permute-start(bf16[224,1024]{1,0:T(8,128)(2,1)S(1)} %shard_map.95.refs_0_.refs_4_), channel_id=1, source_target_pairs={{0,14},{2,0},{4,2},{6,4},{8,6},{10,8},{12,10},{14,12},{1,15},{3,1}... | collective-permute-start | bytes 1376264 | tf_op jit(solution)/shard_map/ppermute | solution.py:28
  8.5 2.0 %copy-done.2 = bf16[1,512,3584]{2,1,0:T(8,128)(2,1)S(1)} copy-done((bf16[1,512,3584]{2,1,0:T(8,128)(2,1)S(1)}, bf16[1,512,3584]{2,1,0:T(8,128)(2,1)}, u32[]{:S(2)}) %copy-start.2) | copy-done | bytes 3670040
  11.2 4.5 %shard_map.93 = (bf16[16,512,224]{2,1,0:T(8,128)(2,1)S(1)}, f32[512,1]{1,0:T(8,128)S(1)}, bf16[224,1024]{1,0:T(8,128)(2,1)S(1)}, bf16[448,1024]{1,0:T(8,128)(2,1)S(1)}, bf16[224,1024]{1,0:T(8,128)(2,1)S(1)}) custom-call(bf16[512,3584]{1,0:T(8,128)(2,1)S(1)} %bitcast.10, f32[28,128]{1,0:T(8,128)S(1)} %bitcast.18, bf16[512,1024]{1,0:T(8,128)(2,1)S(1)} %bitcast.12), custom_call_target="tpu_custom_call" | custom-call | flops 939524096 | bytes 11534336 | tf_op jit(solution)/shard_map/pallas_call | solution.py:61
  19.7 2.4 %collective-permute-start.8 = (bf16[448,1024]{1,0:T(8,128)(2,1)S(1)}, bf16[448,1024]{1,0:T(8,128)(2,1)S(1)}, u32[]{:S(2)}, u32[]{:S(2)}) collective-permute-start(bf16[448,1024]{1,0:T(8,128)(2,1)S(1)} %get-tuple-element.57), channel_id=1, source_target_pairs={{0,14},{2,0},{4,2},{6,4},{8,6},{10,8},{12,10},{14,12},{1,15},{3,1}... | collective-permute-start | bytes 2752520 | tf_op jit(solution)/shard_map/ppermute | solution.py:28
  22.1 5.4 %collective-permute-done.3 = bf16[224,1024]{1,0:T(8,128)(2,1)S(1)} collective-permute-done((bf16[224,1024]{1,0:T(8,128)(2,1)S(1)}, bf16[224,1024]{1,0:T(8,128)(2,1)S(1)}, u32[]{:S(2)}, u32[]{:S(2)}) %collective-permute-start.3) | collective-permute-done | bytes 458784 | tf_op jit(solution)/shard_map/ppermute | solution.py:32
  31.5 3.1 %shard_map.94 = (bf16[448,1024]{1,0:T(8,128)(2,1)S(1)}, bf16[672,1024]{1,0:T(8,128)(2,1)S(1)}, bf16[448,1024]{1,0:T(8,128)(2,1)S(1)}, bf16[448,1024]{1,0:T(8,128...) custom-call(bf16[16,512,224]{2,1,0:T(8,128)(2,1)S(1)} %get-tuple-element.78.blocks.refs_2_, ...), custom_call_target="tpu_custom_call" | custom-call | flops 2818572288 | bytes 11534336 | tf_op jit(solution)/shard_map/pallas_call | solution.py:61
  34.6 11.1 %collective-permute-done.10 = bf16[112,1024]{1,0:T(8,128)(2,1)S(1)} collective-permute-done((bf16[112,1024]{1,0:T(8,128)(2,1)S(1)}, bf16[112,1024]{1,0:T(8,128)(2,1)S(1)}, u32[]{:S(2)}, u32[]{:S(2)}) %collective-permute-start.10) | collective-permute-done | bytes 229408 | tf_op jit(solution)/shard_map/ppermute | solution.py:28
  52.3 18.7 %collective-permute-done.15.refs_6_.refs_10_ = bf16[448,1024]{1,0:T(8,128)(2,1)S(1)} collective-permute-done((bf16[448,1024]{1,0:T(8,128)(2,1)S(1)}, bf16[448,1024]{1,0:T(8,128)(2,1)S(1)}, u32[]{:S(2)}, u32[]{:S(2)}) %collective-permute-start.15) | collective-permute-done | bytes 917536 | tf_op jit(solution)/shard_map/ppermute | solution.py:24
  72.2 1.8 %collective-permute-start.14 = (bf16[224,1024]{1,0:T(8,128)(2,1)S(1)}, bf16[224,1024]{1,0:T(8,128)(2,1)S(1)}, u32[]{:S(2)}, u32[]{:S(2)}) collective-permute-start(bf16[224,1024]{1,0:T(8,128)(2,1)S(1)} %get-tuple-element.69), channel_id=1, source_target_pairs={{0,14},{2,0},{4,2},{6,4},{8,6},{10,8},{12,10},{14,12},{1,15},{3,1}... | collective-permute-start | bytes 1376264 | tf_op jit(solution)/shard_map/ppermute | solution.py:28
  74.7 3.5 %collective-permute-done.13 = bf16[224,1024]{1,0:T(8,128)(2,1)S(1)} collective-permute-done((bf16[224,1024]{1,0:T(8,128)(2,1)S(1)}, bf16[224,1024]{1,0:T(8,128)(2,1)S(1)}, u32[]{:S(2)}, u32[]{:S(2)}) %collective-permute-start.13) | collective-permute-done | bytes 458784 | tf_op jit(solution)/shard_map/ppermute | solution.py:24
  78.2 7.5 %collective-permute-done.14 = bf16[224,1024]{1,0:T(8,128)(2,1)S(1)} collective-permute-done((bf16[224,1024]{1,0:T(8,128)(2,1)S(1)}, bf16[224,1024]{1,0:T(8,128)(2,1)S(1)}, u32[]{:S(2)}, u32[]{:S(2)}) %collective-permute-start.14) | collective-permute-done | bytes 458784 | tf_op jit(solution)/shard_map/ppermute | solution.py:28
  87.1 2.4 %collective-permute-start.19 = (bf16[224,1024]{1,0:T(8,128)(2,1)S(1)}, bf16[224,1024]{1,0:T(8,128)(2,1)S(1)}, u32[]{:S(2)}, u32[]{:S(2)}) collective-permute-start(bf16[224,1024]{1,0:T(8,128)(2,1)S(1)} %get-tuple-element.71), channel_id=1, source_target_pairs={{0,14},{2,0},{4,2},{6,4},{8,6},{10,8},{12,10},{14,12},{1,15},{3,1}... | collective-permute-start | bytes 1376264 | tf_op jit(solution)/shard_map/ppermute | solution.py:28
  89.6 3.4 %shard_map.96.refs_3_ = f32[512,1024]{1,0:T(8,128)S(1)} custom-call(bf16[16,512,224]{2,1,0:T(8,128)(2,1)S(1)} %get-tuple-element.78.blocks.refs_2_, bf16[224,1024]{1,0:T(8,128)(2,1)S(1)} %shard_map.95.refs_0_.refs_4_, bf16[224,1024]{1,0:T(8,128)(2,1)S(1)} %collective-permute-done.5.refs_1_.refs_5_, ...), custom_call_target="tpu_custom_call" | custom-call | flops 2818572288 | bytes 12582912 | tf_op jit(solution)/shard_map/pallas_call | solution.py:61
  93.0 5.4 %collective-permute-done.21.refs_13_ = bf16[336,1024]{1,0:T(8,128)(2,1)S(1)} collective-permute-done((bf16[336,1024]{1,0:T(8,128)(2,1)S(1)}, bf16[336,1024]{1,0:T(8,128)(2,1)S(1)}, u32[]{:S(2)}, u32[]{:S(2)}) %collective-permute-start.21) | collective-permute-done | bytes 688160 | tf_op jit(solution)/shard_map/ppermute | solution.py:28
  100.8 3.2 %collective-permute-done.18 = bf16[224,1024]{1,0:T(8,128)(2,1)S(1)} collective-permute-done((bf16[224,1024]{1,0:T(8,128)(2,1)S(1)}, bf16[224,1024]{1,0:T(8,128)(2,1)S(1)}, u32[]{:S(2)}, u32[]{:S(2)}) %collective-permute-start.18) | collective-permute-done | bytes 458784 | tf_op jit(solution)/shard_map/ppermute | solution.py:24
  105.8 3.1 %collective-permute-start.24 = (bf16[224,1024]{1,0:T(8,128)(2,1)}, bf16[224,1024]{1,0:T(8,128)(2,1)}, u32[]{:S(2)}, u32[]{:S(2)}) collective-permute-start(bf16[224,1024]{1,0:T(8,128)(2,1)} %get-tuple-element.77), channel_id=1, source_target_pairs={{0,14},{2,0},{4,2},{6,4},{8,6},{10,8},{12,10},{14,12},{1,15},{3,1}... | collective-permute-start | bytes 1376264 | tf_op jit(solution)/shard_map/ppermute | solution.py:28
  109.7 2.2 %copy-done.1 = bf16[16,512,224]{2,1,0:T(8,128)(2,1)S(1)} copy-done((bf16[16,512,224]{2,1,0:T(8,128)(2,1)S(1)}, bf16[16,512,224]{2,1,0:T(8,128)(2,1)}, u32[]{:S(2)}) %copy-start.1) | copy-done | bytes 3670040
  111.8 2.0 %copy-done.3 = bf16[1,512,3584]{2,1,0:T(8,128)(2,1)S(1)} copy-done((bf16[1,512,3584]{2,1,0:T(8,128)(2,1)S(1)}, bf16[1,512,3584]{2,1,0:T(8,128)(2,1)}, u32[]{:S(2)}) %copy-start.3) | copy-done | bytes 3670040
  124.9 14.5 %shard_map.97 = (bf16[512,1024]{1,0:T(8,128)(2,1)}, bf16[512,3584]{1,0:T(8,128)(2,1)}) custom-call(f32[28,128]{1,0:T(8,128)S(1)} %bitcast.19, f32[512,1]{1,0:T(8,128)S(1)} %copy-done.30, bf16[512,3584]{1,0:T(8,128)(2,1)S(1)} %bitcast.11, bf16[512,1024]{1,0:T(8,128)(2,1)S(1)} %bitcast.14, bf16[16,512,224]{2,1,0:T(8,128)(2,1)S(1)} %copy-done.1, ...), custom_call_target="tpu_custom_call" | custom-call | flops 4697620480 | bytes 20971520 | tf_op jit(solution)/shard_map/pallas_call | solution.py:61
  139.4 2.4 %shard_map.98 = (f32[224,1024]{1,0:T(8,128)}, f32[224,1024]{1,0:T(8,128)S(1)}, bf16[224,1024]{1,0:T(8,128)(2,1)S(1)}) custom-call(bf16[224,1024]{1,0:T(8,128)(2,1)S(1)} %copy-done.28, bf16[672,1024]{1,0:T(8,128)(2,1)S(1)} %copy-done.15, bf16[224,1024]{1,0:T(8,128)(2,1)} %collective-permute-done.23.rising, bf16[224,1024]{1,0:T(8,128)(2,1)} %collective-permute-done.24.falling, ...), custom_call_target="tpu_custom_call" | custom-call | bytes 6291456 | tf_op jit(solution)/shard_map/pallas_call | solution.py:61
  141.7 1.9 %conditional.1 = (bf16[224,1024]{1,0:T(8,128)(2,1)}) conditional(s32[]{:T(128)} %clamp.3, bf16[224,1024]{1,0:T(8,128)(2,1)S(1)} %get-tuple-element.85, bf16[224,1024]{1,0:T(8,128)(2,1)S(1)} %get-tuple-element.85, bf16[224,1024]{1,0:T(8,128)(2,1)S(1)} %get-tuple-element.85), branch_computations={%region_0.1_spmd, %region_1.2_spmd, %region_2.3_spmd} | conditional | bytes 1835056 | solution.py:325
  141.7 1.9 %collective-permute-done = bf16[224,1024]{1,0:T(8,128)(2,1)} collective-permute-done((bf16[224,1024]{1,0:T(8,128)(2,1)S(1)}, bf16[224,1024]{1,0:T(8,128)(2,1)}, u32[]{:S(2)}, u32[]{:S(2)}) %collective-permute-start) | collective-permute-done | bytes 458784 | tf_op jit(solution)/shard_map/cond/branch_0_fun/ppermute | solution.py:38
  143.7 2.0 %shard_map.99 = f32[224,1024]{1,0:T(8,128)} custom-call(f32[224,1024]{1,0:T(8,128)S(1)} %get-tuple-element.83.updated, bf16[224,1024]{1,0:T(8,128)(2,1)} %get-tuple-element.97.peer), custom_call_target="tpu_custom_call" | custom-call | bytes 2097152 | tf_op jit(solution)/shard_map/pallas_call | solution.py:61
  (107 shorter events, 35.5 us)
Async XLA Ops:
  2.0 87.6 %copy-start.12 = (bf16[224,1024]{1,0:T(8,128)(2,1)}, bf16[224,1024]{1,0:T(8,128)(2,1)S(1)}, u32[]{:S(2)}) copy-start(bf16[224,1024]{1,0:T(8,128)(2,1)S(1)} %shard_map.95.refs_0_.refs_4_) | copy-start | bytes 1376260
  2.0 16.5 %collective-permute-start.4 = (bf16[224,1024]{1,0:T(8,128)(2,1)S(1)}, bf16[224,1024]{1,0:T(8,128)(2,1)S(1)}, u32[]{:S(2)}, u32[]{:S(2)}) collective-permute-start(bf16[224,1024]{1,0:T(8,128)(2,1)S(1)} %shard_map.95.refs_0_.refs_4_), channel_id=1, source_target_pairs={{0,2},{2,4},{4,6},{6,8},{8,10},{10,12},{12,14},{14,0},{1,3},{3,5},... | collective-permute-start | bytes 1376264 | tf_op jit(solution)/shard_map/ppermute | solution.py:24
  4.0 14.5 %collective-permute-start.5 = (bf16[224,1024]{1,0:T(8,128)(2,1)S(1)}, bf16[224,1024]{1,0:T(8,128)(2,1)S(1)}, u32[]{:S(2)}, u32[]{:S(2)}) collective-permute-start(bf16[224,1024]{1,0:T(8,128)(2,1)S(1)} %shard_map.95.refs_0_.refs_4_), channel_id=1, source_target_pairs={{0,1},{1,0},{2,3},{3,2},{4,5},{5,4},{6,7},{7,6},{8,9},{9,8},{10,11... | collective-permute-start | bytes 1376264 | tf_op jit(solution)/shard_map/ppermute | solution.py:32
  4.4 14.0 %collective-permute-start.6 = (bf16[224,1024]{1,0:T(8,128)(2,1)S(1)}, bf16[224,1024]{1,0:T(8,128)(2,1)S(1)}, u32[]{:S(2)}, u32[]{:S(2)}) collective-permute-start(bf16[224,1024]{1,0:T(8,128)(2,1)S(1)} %shard_map.95.refs_0_.refs_4_), channel_id=1, source_target_pairs={{0,14},{2,0},{4,2},{6,4},{8,6},{10,8},{12,10},{14,12},{1,15},{3,1}... | collective-permute-start | bytes 1376264 | tf_op jit(solution)/shard_map/ppermute | solution.py:28
  15.7 11.8 %collective-permute-start.3 = (bf16[224,1024]{1,0:T(8,128)(2,1)S(1)}, bf16[224,1024]{1,0:T(8,128)(2,1)S(1)}, u32[]{:S(2)}, u32[]{:S(2)}) collective-permute-start(bf16[224,1024]{1,0:T(8,128)(2,1)S(1)} %get-tuple-element.51), channel_id=1, source_target_pairs={{0,1},{1,0},{2,3},{3,2},{4,5},{5,4},{6,7},{7,6},{8,9},{9,8},{10,11... | collective-permute-start | bytes 1376264 | tf_op jit(solution)/shard_map/ppermute | solution.py:32
  18.7 27.7 %collective-permute-start.7 = (bf16[448,1024]{1,0:T(8,128)(2,1)S(1)}, bf16[448,1024]{1,0:T(8,128)(2,1)S(1)}, u32[]{:S(2)}, u32[]{:S(2)}) collective-permute-start(bf16[448,1024]{1,0:T(8,128)(2,1)S(1)} %get-tuple-element.56), channel_id=1, source_target_pairs={{0,2},{2,4},{4,6},{6,8},{8,10},{10,12},{12,14},{14,0},{1,3},{3,5},... | collective-permute-start | bytes 2752520 | tf_op jit(solution)/shard_map/ppermute | solution.py:24
  19.7 26.8 %collective-permute-start.8 = (bf16[448,1024]{1,0:T(8,128)(2,1)S(1)}, bf16[448,1024]{1,0:T(8,128)(2,1)S(1)}, u32[]{:S(2)}, u32[]{:S(2)}) collective-permute-start(bf16[448,1024]{1,0:T(8,128)(2,1)S(1)} %get-tuple-element.57), channel_id=1, source_target_pairs={{0,14},{2,0},{4,2},{6,4},{8,6},{10,8},{12,10},{14,12},{1,15},{3,1}... | collective-permute-start | bytes 2752520 | tf_op jit(solution)/shard_map/ppermute | solution.py:28
  27.7 23.4 %collective-permute-start.12 = (bf16[448,1024]{1,0:T(8,128)(2,1)S(1)}, bf16[448,1024]{1,0:T(8,128)(2,1)S(1)}, u32[]{:S(2)}, u32[]{:S(2)}) collective-permute-start(bf16[448,1024]{1,0:T(8,128)(2,1)S(1)} %get-tuple-element.65), channel_id=1, source_target_pairs={{0,1},{1,0},{2,3},{3,2},{4,5},{5,4},{6,7},{7,6},{8,9},{9,8},{10,11... | collective-permute-start | bytes 2752520 | tf_op jit(solution)/shard_map/ppermute | solution.py:32
  29.4 16.3 %collective-permute-start.10 = (bf16[112,1024]{1,0:T(8,128)(2,1)S(1)}, bf16[112,1024]{1,0:T(8,128)(2,1)S(1)}, u32[]{:S(2)}, u32[]{:S(2)}) collective-permute-start(bf16[112,1024]{1,0:T(8,128)(2,1)S(1)} %get-tuple-element.93), channel_id=1, source_target_pairs={{0,14},{2,0},{4,2},{6,4},{8,6},{10,8},{12,10},{14,12},{1,15},{3,1}... | collective-permute-start | bytes 688136 | tf_op jit(solution)/shard_map/ppermute | solution.py:28
  31.1 15.3 %collective-permute-start.9 = (bf16[112,1024]{1,0:T(8,128)(2,1)S(1)}, bf16[112,1024]{1,0:T(8,128)(2,1)S(1)}, u32[]{:S(2)}, u32[]{:S(2)}) collective-permute-start(bf16[112,1024]{1,0:T(8,128)(2,1)S(1)} %get-tuple-element.94), channel_id=1, source_target_pairs={{0,2},{2,4},{4,6},{6,8},{8,10},{10,12},{12,14},{14,0},{1,3},{3,5},... | collective-permute-start | bytes 688136 | tf_op jit(solution)/shard_map/ppermute | solution.py:24
  46.5 24.6 %collective-permute-start.15 = (bf16[448,1024]{1,0:T(8,128)(2,1)S(1)}, bf16[448,1024]{1,0:T(8,128)(2,1)S(1)}, u32[]{:S(2)}, u32[]{:S(2)}) collective-permute-start(bf16[448,1024]{1,0:T(8,128)(2,1)S(1)} %collective-permute-done.7.refs_4_.refs_8_), channel_id=1, source_target_pairs={{0,2},{2,4},{4,6},{6,8},{8,10},{10,12},{12,14},{14,0},{1,3},{3,5},... | collective-permute-start | bytes 2752520 | tf_op jit(solution)/shard_map/ppermute | solution.py:24
  48.2 22.8 %collective-permute-start.16 = (bf16[448,1024]{1,0:T(8,128)(2,1)S(1)}, bf16[448,1024]{1,0:T(8,128)(2,1)S(1)}, u32[]{:S(2)}, u32[]{:S(2)}) collective-permute-start(bf16[448,1024]{1,0:T(8,128)(2,1)S(1)} %collective-permute-done.8.refs_5_.refs_9_), channel_id=1, source_target_pairs={{0,14},{2,0},{4,2},{6,4},{8,6},{10,8},{12,10},{14,12},{1,15},{3,1}... | collective-permute-start | bytes 2752520 | tf_op jit(solution)/shard_map/ppermute | solution.py:28
  49.8 35.9 %collective-permute-start.11 = (bf16[448,1024]{1,0:T(8,128)(2,1)S(1)}, bf16[448,1024]{1,0:T(8,128)(2,1)S(1)}, u32[]{:S(2)}, u32[]{:S(2)}) collective-permute-start(bf16[448,1024]{1,0:T(8,128)(2,1)S(1)} %get-tuple-element.63), channel_id=1, source_target_pairs={{0,1},{1,0},{2,3},{3,2},{4,5},{5,4},{6,7},{7,6},{8,9},{9,8},{10,11... | collective-permute-start | bytes 2752520 | tf_op jit(solution)/shard_map/ppermute | solution.py:32
  51.5 26.7 %collective-permute-start.13 = (bf16[224,1024]{1,0:T(8,128)(2,1)S(1)}, bf16[224,1024]{1,0:T(8,128)(2,1)S(1)}, u32[]{:S(2)}, u32[]{:S(2)}) collective-permute-start(bf16[224,1024]{1,0:T(8,128)(2,1)S(1)} %get-tuple-element.68), channel_id=1, source_target_pairs={{0,2},{2,4},{4,6},{6,8},{8,10},{10,12},{12,14},{14,0},{1,3},{3,5},... | collective-permute-start | bytes 1376264 | tf_op jit(solution)/shard_map/ppermute | solution.py:24
  71.0 33.1 %collective-permute-start.17 = (bf16[672,1024]{1,0:T(8,128)(2,1)S(1)}, bf16[672,1024]{1,0:T(8,128)(2,1)S(1)}, u32[]{:S(2)}, u32[]{:S(2)}) collective-permute-start(bf16[672,1024]{1,0:T(8,128)(2,1)S(1)} %get-tuple-element.75), channel_id=1, source_target_pairs={{0,1},{1,0},{2,3},{3,2},{4,5},{5,4},{6,7},{7,6},{8,9},{9,8},{10,11... | collective-permute-start | bytes 4128776 | tf_op jit(solution)/shard_map/ppermute | solution.py:32
  72.2 13.5 %collective-permute-start.14 = (bf16[224,1024]{1,0:T(8,128)(2,1)S(1)}, bf16[224,1024]{1,0:T(8,128)(2,1)S(1)}, u32[]{:S(2)}, u32[]{:S(2)}) collective-permute-start(bf16[224,1024]{1,0:T(8,128)(2,1)S(1)} %get-tuple-element.69), channel_id=1, source_target_pairs={{0,14},{2,0},{4,2},{6,4},{8,6},{10,8},{12,10},{14,12},{1,15},{3,1}... | collective-permute-start | bytes 1376264 | tf_op jit(solution)/shard_map/ppermute | solution.py:28
  74.1 24.2 %collective-permute-start.21 = (bf16[336,1024]{1,0:T(8,128)(2,1)S(1)}, bf16[336,1024]{1,0:T(8,128)(2,1)S(1)}, u32[]{:S(2)}, u32[]{:S(2)}) collective-permute-start(bf16[336,1024]{1,0:T(8,128)(2,1)S(1)} %slice.79), channel_id=1, source_target_pairs={{0,14},{2,0},{4,2},{6,4},{8,6},{10,8},{12,10},{14,12},{1,15},{3,1}... | collective-permute-start | bytes 2064392 | tf_op jit(solution)/shard_map/ppermute | solution.py:28
  78.2 20.2 %collective-permute-start.20 = (bf16[336,1024]{1,0:T(8,128)(2,1)S(1)}, bf16[336,1024]{1,0:T(8,128)(2,1)S(1)}, u32[]{:S(2)}, u32[]{:S(2)}) collective-permute-start(bf16[336,1024]{1,0:T(8,128)(2,1)S(1)} %slice.78), channel_id=1, source_target_pairs={{0,2},{2,4},{4,6},{6,8},{8,10},{10,12},{12,14},{14,0},{1,3},{3,5},... | collective-permute-start | bytes 2064392 | tf_op jit(solution)/shard_map/ppermute | solution.py:24
  86.2 17.8 %collective-permute-start.18 = (bf16[224,1024]{1,0:T(8,128)(2,1)S(1)}, bf16[224,1024]{1,0:T(8,128)(2,1)S(1)}, u32[]{:S(2)}, u32[]{:S(2)}) collective-permute-start(bf16[224,1024]{1,0:T(8,128)(2,1)S(1)} %get-tuple-element.70), channel_id=1, source_target_pairs={{0,2},{2,4},{4,6},{6,8},{8,10},{10,12},{12,14},{14,0},{1,3},{3,5},... | collective-permute-start | bytes 1376264 | tf_op jit(solution)/shard_map/ppermute | solution.py:24
  87.1 16.9 %collective-permute-start.19 = (bf16[224,1024]{1,0:T(8,128)(2,1)S(1)}, bf16[224,1024]{1,0:T(8,128)(2,1)S(1)}, u32[]{:S(2)}, u32[]{:S(2)}) collective-permute-start(bf16[224,1024]{1,0:T(8,128)(2,1)S(1)} %get-tuple-element.71), channel_id=1, source_target_pairs={{0,14},{2,0},{4,2},{6,4},{8,6},{10,8},{12,10},{14,12},{1,15},{3,1}... | collective-permute-start | bytes 1376264 | tf_op jit(solution)/shard_map/ppermute | solution.py:28
  99.4 10.3 %collective-permute-start.22 = (bf16[224,1024]{1,0:T(8,128)(2,1)}, bf16[224,1024]{1,0:T(8,128)(2,1)}, u32[]{:S(2)}, u32[]{:S(2)}) collective-permute-start(bf16[224,1024]{1,0:T(8,128)(2,1)} %pad_maximum_fusion.2), channel_id=1, source_target_pairs={{0,1},{1,0},{2,3},{3,2},{4,5},{5,4},{6,7},{7,6},{8,9},{9,8},{10,11... | collective-permute-start | bytes 1376264 | tf_op jit(solution)/shard_map/ppermute | solution.py:32
  105.6 33.7 %collective-permute-start.23 = (bf16[224,1024]{1,0:T(8,128)(2,1)}, bf16[224,1024]{1,0:T(8,128)(2,1)}, u32[]{:S(2)}, u32[]{:S(2)}) collective-permute-start(bf16[224,1024]{1,0:T(8,128)(2,1)} %get-tuple-element.76), channel_id=1, source_target_pairs={{0,2},{2,4},{4,6},{6,8},{8,10},{10,12},{12,14},{14,0},{1,3},{3,5},... | collective-permute-start | bytes 1376264 | tf_op jit(solution)/shard_map/ppermute | solution.py:24
  105.8 33.5 %collective-permute-start.24 = (bf16[224,1024]{1,0:T(8,128)(2,1)}, bf16[224,1024]{1,0:T(8,128)(2,1)}, u32[]{:S(2)}, u32[]{:S(2)}) collective-permute-start(bf16[224,1024]{1,0:T(8,128)(2,1)} %get-tuple-element.77), channel_id=1, source_target_pairs={{0,14},{2,0},{4,2},{6,4},{8,6},{10,8},{12,10},{14,12},{1,15},{3,1}... | collective-permute-start | bytes 1376264 | tf_op jit(solution)/shard_map/ppermute | solution.py:28
  141.7 1.9 %collective-permute-start = (bf16[224,1024]{1,0:T(8,128)(2,1)S(1)}, bf16[224,1024]{1,0:T(8,128)(2,1)}, u32[]{:S(2)}, u32[]{:S(2)}) collective-permute-start(bf16[224,1024]{1,0:T(8,128)(2,1)S(1)} %param), channel_id=1, source_target_pairs={{0,16},{16,0},{32,48},{48,32},{64,80},{80,64},{96,112},{112,96},{1... | collective-permute-start | bytes 1376264 | tf_op jit(solution)/shard_map/cond/branch_0_fun/ppermute | solution.py:38
  (32 other events, 478.8 us)

commit v2 on v0

--- a/solution.py
+++ b/solution.py
@@ -14,6 +14,9 @@
 FIRST = ((4, 1), (3, 1), (-3, 1), (4, 0))
 SECOND = ((2, 1), (-2, 1), (1, 1), (-1, 1), (0, 1))
 SECOND += ((3, 0), (-3, 0), (2, 0), (-2, 0), (1, 0), (-1, 0), (0, 0))
+
+
+LAST = ((-3, 1), (3, 1), (4, 0), (4, 1))
 
 
 def ring(n, by):
@@ -163,21 +166,18 @@
 
 
 def near_keys_kernel(blocks, *refs):
-    gathered, out = refs[:8], refs[8]
+    gathered, out, kept = refs[:8], refs[8], refs[9]
+    for i, (by, column) in enumerate(LAST):
+        kept[i] = blocks[shard_at(by, column)]
     wanted = [piece for piece in pieces(blocks.shape[2]) if piece[0] < 8]
     shards = [(shard_at(by, column), gathered[i], at) for i, at, _, by, column, _ in wanted]
     add_products(blocks, shards, None, out, 1.0)
 
 
-def far_keys_kernel(blocks, near, up4, down4, far, far_other, out):
-    part = blocks.shape[2]
-    shards = [
-        (shard_at(-3, 1), up4, part // 2),
-        (shard_at(3, 1), down4, 0),
-        (shard_at(4, 0), far, 0),
-        (shard_at(4, 1), far_other, 0),
-    ]
-    add_products(blocks, shards, near, out, (16 * part) ** (-0.5))
+def far_keys_kernel(kept, near, up4, down4, far, far_other, out):
+    part = kept.shape[2]
+    shards = [(0, up4, part // 2), (1, down4, 0), (2, far, 0), (3, far_other, 0)]
+    add_products(kept, shards, near, out, (16 * part) ** (-0.5))
 
 
 def input_kernel(gain, inverse, cot, tokens, *refs):
@@ -281,10 +281,10 @@
     plus, minus = reduced(own2, second, rising, falling, up3, down3)
     rising, falling = up(plus), down(minus)
     blocks = after(blocks, plus, minus)
-    (near,) = call(
+    near, kept = call(
         near_keys_kernel,
         [blocks, own, other, up1, down1, up2, down2, up3, down3],
-        [((rows, features), f32)],
+        [((rows, features), f32), ((4, rows, part), bf16)],
         flops=12 * product,
         moved=12 * 2**20,
     )
@@ -295,7 +295,7 @@
 
     (keys,) = call(
         far_keys_kernel,
-        [after(blocks, plus, minus), near, up4, down4, far_rows, far_other],
+        [after(kept, plus, minus), near, up4, down4, far_rows, far_other],
         [((rows, features), bf16)],
         flops=4 * product,
         moved=9 * 2**20,

time: 146 us -> 146 us (level)
  waiting for transfers between devices: 67.8 us -> 62.7 us
  local copies, waits for them, and re-layouts: 11.3 us -> 15.5 us
  starting transfers between devices: 34.1 us -> 36.4 us
    ppermute x8, waiting for transfers between devices: 24 us -> 6.87 us  [down(): return lax.ppermute(value, 'z', ring(lax.axis_size('z'), -1))]
    ppermute x8, waiting for transfers between devices: 28.3 us -> 40.2 us  [up(): return lax.ppermute(value, 'z', ring(lax.axis_size('z'), 1))]
    unnamed x70 -> x66, local copies, waits for them, and re-layouts: 11.2 us -> 15.4 us
    ppermute x8, starting transfers between devices: 1.02 us -> 3.07 us  [up(): return lax.ppermute(value, 'z', ring(lax.axis_size('z'), 1))]
    ppermute x1, starting transfers between devices: 3.02 us -> 1.49 us  [swapped(): return lax.ppermute(value, 'rep', pairs)]
    ppermute x8, starting transfers between devices: 24.2 us -> 25.7 us  [down(): return lax.ppermute(value, 'z', ring(lax.axis_size('z'), -1))]
  transfers between devices with their start and end apart: 23 -> 23, of which waited for: 13 -> 12; matrix products, arithmetic and copies ran while one was open for 3% -> 3% of each run, Pallas kernels for 16% -> 16%
where the time goes in v2:
time: 146 us; the launch traced here: 148 us
  waiting for transfers between devices  62.7 us (43%)
  starting transfers between devices  36.4 us (25%)
  Pallas kernels  27.9 us (19%)
  local copies, waits for them, and re-layouts  15.5 us (11%)
  other arithmetic  3.72 us (3%)
  between operations  1.65 us (1%)
    ppermute x8, waiting for transfers between devices, up(): return lax.ppermute(value, 'z', ring(lax.axis_size('z'), 1))  40.2 us
    pallas_call x8, Pallas kernels, call(): pl.pallas_call(kernel, in_specs=[vmem] * (len(inputs) - anywhere) + [free...  27.9 us
    ppermute x8, starting transfers between devices, down(): return lax.ppermute(value, 'z', ring(lax.axis_size('z'), -1))  25.7 us
    unnamed x66, local copies, waits for them, and re-layouts  15.4 us
    ppermute x6, waiting for transfers between devices, across(): return lax.ppermute(value, 'y', [(0, 1), (1, 0)])  8.47 us
    ppermute x1, waiting for transfers between devices, swapped(): return lax.ppermute(value, 'rep', pairs)  7.09 us
    ppermute x8, waiting for transfers between devices, down(): return lax.ppermute(value, 'z', ring(lax.axis_size('z'), -1))  6.87 us
    ppermute x6, starting transfers between devices, across(): return lax.ppermute(value, 'y', [(0, 1), (1, 0)])  6.17 us
  transfers between devices with their start and end apart: 23, of which 12 were waited for; matrix products, arithmetic and copies ran while one was open for 3% of the time, Pallas kernels for 16%

profile of v2, /device:TPU:8, one launch (start us, length us, event | category | flops | bytes accessed | tf_op | source)
XLA Modules:
  0.0 147.9 jit_solution(3915452471459088075)
XLA Ops:
  2.0 5.9 %collective-permute-start.6 = (bf16[224,1024]{1,0:T(8,128)(2,1)S(1)}, bf16[224,1024]{1,0:T(8,128)(2,1)S(1)}, u32[]{:S(2)}, u32[]{:S(2)}) collective-permute-start(bf16[224,1024]{1,0:T(8,128)(2,1)S(1)} %shard_map.95.refs_0_), channel_id=1, source_target_pairs={{0,14},{2,0},{4,2},{6,4},{8,6},{10,8},{12,10},{14,12},{1,15},{3,1}... | collective-permute-start | bytes 1376264 | tf_op jit(solution)/shard_map/ppermute | solution.py:31
  11.1 4.5 %shard_map.93 = (bf16[16,512,224]{2,1,0:T(8,128)(2,1)S(1)}, f32[512,1]{1,0:T(8,128)S(1)}, bf16[224,1024]{1,0:T(8,128)(2,1)S(1)}, bf16[448,1024]{1,0:T(8,128)(2,1)S(1)}, bf16[224,1024]{1,0:T(8,128)(2,1)S(1)}) custom-call(bf16[512,3584]{1,0:T(8,128)(2,1)S(1)} %bitcast.10, f32[28,128]{1,0:T(8,128)S(1)} %bitcast.18, bf16[512,1024]{1,0:T(8,128)(2,1)S(1)} %bitcast.12), custom_call_target="tpu_custom_call" | custom-call | flops 939524096 | bytes 11534336 | tf_op jit(solution)/shard_map/pallas_call | solution.py:64
  17.7 3.7 %collective-permute-done.5.refs_1_ = bf16[224,1024]{1,0:T(8,128)(2,1)S(1)} collective-permute-done((bf16[224,1024]{1,0:T(8,128)(2,1)S(1)}, bf16[224,1024]{1,0:T(8,128)(2,1)S(1)}, u32[]{:S(2)}, u32[]{:S(2)}) %collective-permute-start.5) | collective-permute-done | bytes 458784 | tf_op jit(solution)/shard_map/ppermute | solution.py:35
  21.7 3.2 %collective-permute-start.8 = (bf16[448,1024]{1,0:T(8,128)(2,1)S(1)}, bf16[448,1024]{1,0:T(8,128)(2,1)S(1)}, u32[]{:S(2)}, u32[]{:S(2)}) collective-permute-start(bf16[448,1024]{1,0:T(8,128)(2,1)S(1)} %get-tuple-element.57), channel_id=1, source_target_pairs={{0,14},{2,0},{4,2},{6,4},{8,6},{10,8},{12,10},{14,12},{1,15},{3,1}... | collective-permute-start | bytes 2752520 | tf_op jit(solution)/shard_map/ppermute | solution.py:31
  24.9 4.8 %collective-permute-done.3 = bf16[224,1024]{1,0:T(8,128)(2,1)S(1)} collective-permute-done((bf16[224,1024]{1,0:T(8,128)(2,1)S(1)}, bf16[224,1024]{1,0:T(8,128)(2,1)S(1)}, u32[]{:S(2)}, u32[]{:S(2)}) %collective-permute-start.3) | collective-permute-done | bytes 458784 | tf_op jit(solution)/shard_map/ppermute | solution.py:35
  30.5 3.2 %collective-permute-start.10 = (bf16[112,1024]{1,0:T(8,128)(2,1)S(1)}, bf16[112,1024]{1,0:T(8,128)(2,1)S(1)}, u32[]{:S(2)}, u32[]{:S(2)}) collective-permute-start(bf16[112,1024]{1,0:T(8,128)(2,1)S(1)} %get-tuple-element.95), channel_id=1, source_target_pairs={{0,14},{2,0},{4,2},{6,4},{8,6},{10,8},{12,10},{14,12},{1,15},{3,1}... | collective-permute-start | bytes 688136 | tf_op jit(solution)/shard_map/ppermute | solution.py:31
  33.8 3.1 %shard_map.94 = (bf16[448,1024]{1,0:T(8,128)(2,1)S(1)}, bf16[672,1024]{1,0:T(8,128)(2,1)S(1)}, bf16[448,1024]{1,0:T(8,128)(2,1)S(1)}, bf16[448,1024]{1,0:T(8,128...) custom-call(bf16[16,512,224]{2,1,0:T(8,128)(2,1)S(1)} %get-tuple-element.72.blocks, ...), custom_call_target="tpu_custom_call" | custom-call | flops 2818572288 | bytes 11534336 | tf_op jit(solution)/shard_map/pallas_call | solution.py:64
  37.6 10.7 %collective-permute-done.9 = bf16[112,1024]{1,0:T(8,128)(2,1)S(1)} collective-permute-done((bf16[112,1024]{1,0:T(8,128)(2,1)S(1)}, bf16[112,1024]{1,0:T(8,128)(2,1)S(1)}, u32[]{:S(2)}, u32[]{:S(2)}) %collective-permute-start.9) | collective-permute-done | bytes 229408 | tf_op jit(solution)/shard_map/ppermute | solution.py:27
  48.4 3.2 %collective-permute-start.16 = (bf16[448,1024]{1,0:T(8,128)(2,1)S(1)}, bf16[448,1024]{1,0:T(8,128)(2,1)S(1)}, u32[]{:S(2)}, u32[]{:S(2)}) collective-permute-start(bf16[448,1024]{1,0:T(8,128)(2,1)S(1)} %collective-permute-done.8.refs_5_), channel_id=1, source_target_pairs={{0,14},{2,0},{4,2},{6,4},{8,6},{10,8},{12,10},{14,12},{1,15},{3,1}... | collective-permute-start | bytes 2752520 | tf_op jit(solution)/shard_map/ppermute | solution.py:31
  55.5 13.7 %collective-permute-done.15.refs_6_ = bf16[448,1024]{1,0:T(8,128)(2,1)S(1)} collective-permute-done((bf16[448,1024]{1,0:T(8,128)(2,1)S(1)}, bf16[448,1024]{1,0:T(8,128)(2,1)S(1)}, u32[]{:S(2)}, u32[]{:S(2)}) %collective-permute-start.15) | collective-permute-done | bytes 917536 | tf_op jit(solution)/shard_map/ppermute | solution.py:27
  69.2 3.2 %collective-permute-done.16.refs_7_ = bf16[448,1024]{1,0:T(8,128)(2,1)S(1)} collective-permute-done((bf16[448,1024]{1,0:T(8,128)(2,1)S(1)}, bf16[448,1024]{1,0:T(8,128)(2,1)S(1)}, u32[]{:S(2)}, u32[]{:S(2)}) %collective-permute-start.16) | collective-permute-done | bytes 917536 | tf_op jit(solution)/shard_map/ppermute | solution.py:31
  74.7 2.1 %collective-permute-start.20 = (bf16[336,1024]{1,0:T(8,128)(2,1)S(1)}, bf16[336,1024]{1,0:T(8,128)(2,1)S(1)}, u32[]{:S(2)}, u32[]{:S(2)}) collective-permute-start(bf16[336,1024]{1,0:T(8,128)(2,1)S(1)} %slice.78), channel_id=1, source_target_pairs={{0,2},{2,4},{4,6},{6,8},{8,10},{10,12},{12,14},{14,0},{1,3},{3,5},... | collective-permute-start | bytes 2064392 | tf_op jit(solution)/shard_map/ppermute | solution.py:27
  76.9 2.2 %collective-permute-done.14 = bf16[224,1024]{1,0:T(8,128)(2,1)S(1)} collective-permute-done((bf16[224,1024]{1,0:T(8,128)(2,1)S(1)}, bf16[224,1024]{1,0:T(8,128)(2,1)S(1)}, u32[]{:S(2)}, u32[]{:S(2)}) %collective-permute-start.14) | collective-permute-done | bytes 458784 | tf_op jit(solution)/shard_map/ppermute | solution.py:31
  79.0 3.0 %collective-permute-start.21 = (bf16[336,1024]{1,0:T(8,128)(2,1)S(1)}, bf16[336,1024]{1,0:T(8,128)(2,1)S(1)}, u32[]{:S(2)}, u32[]{:S(2)}) collective-permute-start(bf16[336,1024]{1,0:T(8,128)(2,1)S(1)} %slice.79), channel_id=1, source_target_pairs={{0,14},{2,0},{4,2},{6,4},{8,6},{10,8},{12,10},{14,12},{1,15},{3,1}... | collective-permute-start | bytes 2064392 | tf_op jit(solution)/shard_map/ppermute | solution.py:31
  82.0 7.2 %collective-permute-done.13 = bf16[224,1024]{1,0:T(8,128)(2,1)S(1)} collective-permute-done((bf16[224,1024]{1,0:T(8,128)(2,1)S(1)}, bf16[224,1024]{1,0:T(8,128)(2,1)S(1)}, u32[]{:S(2)}, u32[]{:S(2)}) %collective-permute-start.13) | collective-permute-done | bytes 458784 | tf_op jit(solution)/shard_map/ppermute | solution.py:27
  91.9 3.4 %shard_map.96 = (f32[512,1024]{1,0:T(8,128)S(1)}, bf16[4,512,224]{2,1,0:T(8,128)(2,1)S(1)}) custom-call(bf16[16,512,224]{2,1,0:T(8,128)(2,1)S(1)} %get-tuple-element.72.blocks, bf16[224,1024]{1,0:T(8,128)(2,1)S(1)} %shard_map.95.refs_0_, bf16[224,1024]{1,0:T(8,128)(2,1)S(1)} %collective-permute-done.5.refs_1_, ...), custom_call_target="tpu_custom_call" | custom-call | flops 2818572288 | bytes 12582912 | tf_op jit(solution)/shard_map/pallas_call | solution.py:64
  95.3 5.2 %collective-permute-done.20.up4.refs_8_ = bf16[336,1024]{1,0:T(8,128)(2,1)S(1)} collective-permute-done((bf16[336,1024]{1,0:T(8,128)(2,1)S(1)}, bf16[336,1024]{1,0:T(8,128)(2,1)S(1)}, u32[]{:S(2)}, u32[]{:S(2)}) %collective-permute-start.20) | collective-permute-done | bytes 688160 | tf_op jit(solution)/shard_map/ppermute | solution.py:27
  102.9 3.4 %collective-permute-done.18 = bf16[224,1024]{1,0:T(8,128)(2,1)S(1)} collective-permute-done((bf16[224,1024]{1,0:T(8,128)(2,1)S(1)}, bf16[224,1024]{1,0:T(8,128)(2,1)S(1)}, u32[]{:S(2)}, u32[]{:S(2)}) %collective-permute-start.18) | collective-permute-done | bytes 458784 | tf_op jit(solution)/shard_map/ppermute | solution.py:27
  107.9 3.2 %collective-permute-start.24 = (bf16[224,1024]{1,0:T(8,128)(2,1)}, bf16[224,1024]{1,0:T(8,128)(2,1)}, u32[]{:S(2)}, u32[]{:S(2)}) collective-permute-start(bf16[224,1024]{1,0:T(8,128)(2,1)} %get-tuple-element.78), channel_id=1, source_target_pairs={{0,14},{2,0},{4,2},{6,4},{8,6},{10,8},{12,10},{14,12},{1,15},{3,1}... | collective-permute-start | bytes 1376264 | tf_op jit(solution)/shard_map/ppermute | solution.py:31
  115.9 3.5 %shard_map.97 = bf16[512,1024]{1,0:T(8,128)(2,1)} custom-call(bf16[4,512,224]{2,1,0:T(8,128)(2,1)S(1)} %copy-done.23, f32[512,1024]{1,0:T(8,128)S(1)} %copy-done.13, bf16[336,1024]{1,0:T(8,128)(2,1)S(1)} %collective-permute-done.20.up4.refs_8_, bf16[336,1024]{1,0:T(8,128)(2,1)S(1)} %copy-done.4, bf16[224,1024]{1,0:T(8,128)(2,1)} %pad_maximum_fusion.2.far, ...), custom_call_target="tpu_custom_call" | custom-call | flops 939524096 | bytes 9437184 | tf_op jit(solution)/shard_map/pallas_call | solution.py:64
  125.9 9.0 %shard_map.98 = bf16[512,3584]{1,0:T(8,128)(2,1)} custom-call(f32[28,128]{1,0:T(8,128)S(1)} %bitcast.19, f32[512,1]{1,0:T(8,128)S(1)} %get-tuple-element.82.inverse, bf16[512,1024]{1,0:T(8,128)(2,1)S(1)} %bitcast.14, bf16[512,3584]{1,0:T(8,128)(2,1)S(1)} %bitcast.11, bf16[224,1024]{1,0:T(8,128)(2,1)S(1)} %copy-done.21, bf16[224,1024]{1,0:T(8,128)(2,1)S(1)} %copy-done.17, ...), custom_call_target="tpu_custom_call" | custom-call | flops 3758096384 | bytes 16777216 | tf_op jit(solution)/shard_map/pallas_call | solution.py:64
  135.0 2.4 %shard_map.99 = (f32[224,1024]{1,0:T(8,128)}, f32[224,1024]{1,0:T(8,128)S(1)}, bf16[224,1024]{1,0:T(8,128)(2,1)S(1)}) custom-call(bf16[224,1024]{1,0:T(8,128)(2,1)S(1)} %copy-done.30, bf16[672,1024]{1,0:T(8,128)(2,1)S(1)} %collective-permute-done.17.first, bf16[224,1024]{1,0:T(8,128)(2,1)} %collective-permute-done.23.rising, ...), custom_call_target="tpu_custom_call" | custom-call | bytes 6291456 | tf_op jit(solution)/shard_map/pallas_call | solution.py:64
  137.3 8.6 %conditional.1 = (bf16[224,1024]{1,0:T(8,128)(2,1)}) conditional(s32[]{:T(128)} %clamp.3, bf16[224,1024]{1,0:T(8,128)(2,1)S(1)} %get-tuple-element.87, bf16[224,1024]{1,0:T(8,128)(2,1)S(1)} %get-tuple-element.87, bf16[224,1024]{1,0:T(8,128)(2,1)S(1)} %get-tuple-element.87), branch_computations={%region_0.1_spmd, %region_1.2_spmd, %region_2.3_spmd} | conditional | bytes 1835056 | solution.py:321
  138.8 7.1 %collective-permute-done.1 = bf16[224,1024]{1,0:T(8,128)(2,1)} collective-permute-done((bf16[224,1024]{1,0:T(8,128)(2,1)S(1)}, bf16[224,1024]{1,0:T(8,128)(2,1)}, u32[]{:S(2)}, u32[]{:S(2)}) %collective-permute-start.1) | collective-permute-done | bytes 458784 | tf_op jit(solution)/shard_map/cond/branch_1_fun/ppermute | solution.py:41
  (108 shorter events, 35.3 us)
Async XLA Ops:
  2.0 89.9 %copy-start.20 = (bf16[224,1024]{1,0:T(8,128)(2,1)}, bf16[224,1024]{1,0:T(8,128)(2,1)S(1)}, u32[]{:S(2)}) copy-start(bf16[224,1024]{1,0:T(8,128)(2,1)S(1)} %shard_map.95.refs_0_) | copy-start | bytes 1376260
  2.0 15.7 %collective-permute-start.6 = (bf16[224,1024]{1,0:T(8,128)(2,1)S(1)}, bf16[224,1024]{1,0:T(8,128)(2,1)S(1)}, u32[]{:S(2)}, u32[]{:S(2)}) collective-permute-start(bf16[224,1024]{1,0:T(8,128)(2,1)S(1)} %shard_map.95.refs_0_), channel_id=1, source_target_pairs={{0,14},{2,0},{4,2},{6,4},{8,6},{10,8},{12,10},{14,12},{1,15},{3,1}... | collective-permute-start | bytes 1376264 | tf_op jit(solution)/shard_map/ppermute | solution.py:31
  7.9 13.4 %collective-permute-start.5 = (bf16[224,1024]{1,0:T(8,128)(2,1)S(1)}, bf16[224,1024]{1,0:T(8,128)(2,1)S(1)}, u32[]{:S(2)}, u32[]{:S(2)}) collective-permute-start(bf16[224,1024]{1,0:T(8,128)(2,1)S(1)} %shard_map.95.refs_0_), channel_id=1, source_target_pairs={{0,1},{1,0},{2,3},{3,2},{4,5},{5,4},{6,7},{7,6},{8,9},{9,8},{10,11... | collective-permute-start | bytes 1376264 | tf_op jit(solution)/shard_map/ppermute | solution.py:35
  8.4 13.0 %collective-permute-start.4 = (bf16[224,1024]{1,0:T(8,128)(2,1)S(1)}, bf16[224,1024]{1,0:T(8,128)(2,1)S(1)}, u32[]{:S(2)}, u32[]{:S(2)}) collective-permute-start(bf16[224,1024]{1,0:T(8,128)(2,1)S(1)} %shard_map.95.refs_0_), channel_id=1, source_target_pairs={{0,2},{2,4},{4,6},{6,8},{8,10},{10,12},{12,14},{14,0},{1,3},{3,5},... | collective-permute-start | bytes 1376264 | tf_op jit(solution)/shard_map/ppermute | solution.py:27
  15.6 14.1 %collective-permute-start.3 = (bf16[224,1024]{1,0:T(8,128)(2,1)S(1)}, bf16[224,1024]{1,0:T(8,128)(2,1)S(1)}, u32[]{:S(2)}, u32[]{:S(2)}) collective-permute-start(bf16[224,1024]{1,0:T(8,128)(2,1)S(1)} %get-tuple-element.51), channel_id=1, source_target_pairs={{0,1},{1,0},{2,3},{3,2},{4,5},{5,4},{6,7},{7,6},{8,9},{9,8},{10,11... | collective-permute-start | bytes 1376264 | tf_op jit(solution)/shard_map/ppermute | solution.py:35
  21.6 26.7 %collective-permute-start.7 = (bf16[448,1024]{1,0:T(8,128)(2,1)S(1)}, bf16[448,1024]{1,0:T(8,128)(2,1)S(1)}, u32[]{:S(2)}, u32[]{:S(2)}) collective-permute-start(bf16[448,1024]{1,0:T(8,128)(2,1)S(1)} %get-tuple-element.56), channel_id=1, source_target_pairs={{0,2},{2,4},{4,6},{6,8},{8,10},{10,12},{12,14},{14,0},{1,3},{3,5},... | collective-permute-start | bytes 2752520 | tf_op jit(solution)/shard_map/ppermute | solution.py:27
  21.7 26.6 %collective-permute-start.8 = (bf16[448,1024]{1,0:T(8,128)(2,1)S(1)}, bf16[448,1024]{1,0:T(8,128)(2,1)S(1)}, u32[]{:S(2)}, u32[]{:S(2)}) collective-permute-start(bf16[448,1024]{1,0:T(8,128)(2,1)S(1)} %get-tuple-element.57), channel_id=1, source_target_pairs={{0,14},{2,0},{4,2},{6,4},{8,6},{10,8},{12,10},{14,12},{1,15},{3,1}... | collective-permute-start | bytes 2752520 | tf_op jit(solution)/shard_map/ppermute | solution.py:31
  29.9 23.4 %collective-permute-start.12 = (bf16[448,1024]{1,0:T(8,128)(2,1)S(1)}, bf16[448,1024]{1,0:T(8,128)(2,1)S(1)}, u32[]{:S(2)}, u32[]{:S(2)}) collective-permute-start(bf16[448,1024]{1,0:T(8,128)(2,1)S(1)} %get-tuple-element.65), channel_id=1, source_target_pairs={{0,1},{1,0},{2,3},{3,2},{4,5},{5,4},{6,7},{7,6},{8,9},{9,8},{10,11... | collective-permute-start | bytes 2752520 | tf_op jit(solution)/shard_map/ppermute | solution.py:35
  30.4 17.9 %collective-permute-start.9 = (bf16[112,1024]{1,0:T(8,128)(2,1)S(1)}, bf16[112,1024]{1,0:T(8,128)(2,1)S(1)}, u32[]{:S(2)}, u32[]{:S(2)}) collective-permute-start(bf16[112,1024]{1,0:T(8,128)(2,1)S(1)} %get-tuple-element.96), channel_id=1, source_target_pairs={{0,2},{2,4},{4,6},{6,8},{8,10},{10,12},{12,14},{14,0},{1,3},{3,5},... | collective-permute-start | bytes 688136 | tf_op jit(solution)/shard_map/ppermute | solution.py:27
  30.5 17.8 %collective-permute-start.10 = (bf16[112,1024]{1,0:T(8,128)(2,1)S(1)}, bf16[112,1024]{1,0:T(8,128)(2,1)S(1)}, u32[]{:S(2)}, u32[]{:S(2)}) collective-permute-start(bf16[112,1024]{1,0:T(8,128)(2,1)S(1)} %get-tuple-element.95), channel_id=1, source_target_pairs={{0,14},{2,0},{4,2},{6,4},{8,6},{10,8},{12,10},{14,12},{1,15},{3,1}... | collective-permute-start | bytes 688136 | tf_op jit(solution)/shard_map/ppermute | solution.py:31
  48.3 20.9 %collective-permute-start.15 = (bf16[448,1024]{1,0:T(8,128)(2,1)S(1)}, bf16[448,1024]{1,0:T(8,128)(2,1)S(1)}, u32[]{:S(2)}, u32[]{:S(2)}) collective-permute-start(bf16[448,1024]{1,0:T(8,128)(2,1)S(1)} %collective-permute-done.7.refs_4_), channel_id=1, source_target_pairs={{0,2},{2,4},{4,6},{6,8},{8,10},{10,12},{12,14},{14,0},{1,3},{3,5},... | collective-permute-start | bytes 2752520 | tf_op jit(solution)/shard_map/ppermute | solution.py:27
  48.4 24.0 %collective-permute-start.16 = (bf16[448,1024]{1,0:T(8,128)(2,1)S(1)}, bf16[448,1024]{1,0:T(8,128)(2,1)S(1)}, u32[]{:S(2)}, u32[]{:S(2)}) collective-permute-start(bf16[448,1024]{1,0:T(8,128)(2,1)S(1)} %collective-permute-done.8.refs_5_), channel_id=1, source_target_pairs={{0,14},{2,0},{4,2},{6,4},{8,6},{10,8},{12,10},{14,12},{1,15},{3,1}... | collective-permute-start | bytes 2752520 | tf_op jit(solution)/shard_map/ppermute | solution.py:31
  51.7 37.5 %collective-permute-start.11 = (bf16[448,1024]{1,0:T(8,128)(2,1)S(1)}, bf16[448,1024]{1,0:T(8,128)(2,1)S(1)}, u32[]{:S(2)}, u32[]{:S(2)}) collective-permute-start(bf16[448,1024]{1,0:T(8,128)(2,1)S(1)} %get-tuple-element.63), channel_id=1, source_target_pairs={{0,1},{1,0},{2,3},{3,2},{4,5},{5,4},{6,7},{7,6},{8,9},{9,8},{10,11... | collective-permute-start | bytes 2752520 | tf_op jit(solution)/shard_map/ppermute | solution.py:35
  53.7 25.4 %collective-permute-start.14 = (bf16[224,1024]{1,0:T(8,128)(2,1)S(1)}, bf16[224,1024]{1,0:T(8,128)(2,1)S(1)}, u32[]{:S(2)}, u32[]{:S(2)}) collective-permute-start(bf16[224,1024]{1,0:T(8,128)(2,1)S(1)} %get-tuple-element.69), channel_id=1, source_target_pairs={{0,14},{2,0},{4,2},{6,4},{8,6},{10,8},{12,10},{14,12},{1,15},{3,1}... | collective-permute-start | bytes 1376264 | tf_op jit(solution)/shard_map/ppermute | solution.py:31
  72.5 33.8 %collective-permute-start.17 = (bf16[672,1024]{1,0:T(8,128)(2,1)S(1)}, bf16[672,1024]{1,0:T(8,128)(2,1)S(1)}, u32[]{:S(2)}, u32[]{:S(2)}) collective-permute-start(bf16[672,1024]{1,0:T(8,128)(2,1)S(1)} %get-tuple-element.76), channel_id=1, source_target_pairs={{0,1},{1,0},{2,3},{3,2},{4,5},{5,4},{6,7},{7,6},{8,9},{9,8},{10,11... | collective-permute-start | bytes 4128776 | tf_op jit(solution)/shard_map/ppermute | solution.py:35
  74.0 15.1 %collective-permute-start.13 = (bf16[224,1024]{1,0:T(8,128)(2,1)S(1)}, bf16[224,1024]{1,0:T(8,128)(2,1)S(1)}, u32[]{:S(2)}, u32[]{:S(2)}) collective-permute-start(bf16[224,1024]{1,0:T(8,128)(2,1)S(1)} %get-tuple-element.68), channel_id=1, source_target_pairs={{0,2},{2,4},{4,6},{6,8},{8,10},{10,12},{12,14},{14,0},{1,3},{3,5},... | collective-permute-start | bytes 1376264 | tf_op jit(solution)/shard_map/ppermute | solution.py:27
  74.7 25.8 %collective-permute-start.20 = (bf16[336,1024]{1,0:T(8,128)(2,1)S(1)}, bf16[336,1024]{1,0:T(8,128)(2,1)S(1)}, u32[]{:S(2)}, u32[]{:S(2)}) collective-permute-start(bf16[336,1024]{1,0:T(8,128)(2,1)S(1)} %slice.78), channel_id=1, source_target_pairs={{0,2},{2,4},{4,6},{6,8},{8,10},{10,12},{12,14},{14,0},{1,3},{3,5},... | collective-permute-start | bytes 2064392 | tf_op jit(solution)/shard_map/ppermute | solution.py:27
  79.0 21.5 %collective-permute-start.21 = (bf16[336,1024]{1,0:T(8,128)(2,1)S(1)}, bf16[336,1024]{1,0:T(8,128)(2,1)S(1)}, u32[]{:S(2)}, u32[]{:S(2)}) collective-permute-start(bf16[336,1024]{1,0:T(8,128)(2,1)S(1)} %slice.79), channel_id=1, source_target_pairs={{0,14},{2,0},{4,2},{6,4},{8,6},{10,8},{12,10},{14,12},{1,15},{3,1}... | collective-permute-start | bytes 2064392 | tf_op jit(solution)/shard_map/ppermute | solution.py:31
  89.7 13.2 %collective-permute-start.19 = (bf16[224,1024]{1,0:T(8,128)(2,1)S(1)}, bf16[224,1024]{1,0:T(8,128)(2,1)S(1)}, u32[]{:S(2)}, u32[]{:S(2)}) collective-permute-start(bf16[224,1024]{1,0:T(8,128)(2,1)S(1)} %get-tuple-element.71), channel_id=1, source_target_pairs={{0,14},{2,0},{4,2},{6,4},{8,6},{10,8},{12,10},{14,12},{1,15},{3,1}... | collective-permute-start | bytes 1376264 | tf_op jit(solution)/shard_map/ppermute | solution.py:31
  91.8 14.5 %collective-permute-start.18 = (bf16[224,1024]{1,0:T(8,128)(2,1)S(1)}, bf16[224,1024]{1,0:T(8,128)(2,1)S(1)}, u32[]{:S(2)}, u32[]{:S(2)}) collective-permute-start(bf16[224,1024]{1,0:T(8,128)(2,1)S(1)} %get-tuple-element.70), channel_id=1, source_target_pairs={{0,2},{2,4},{4,6},{6,8},{8,10},{10,12},{12,14},{14,0},{1,3},{3,5},... | collective-permute-start | bytes 1376264 | tf_op jit(solution)/shard_map/ppermute | solution.py:27
  101.5 10.2 %collective-permute-start.22 = (bf16[224,1024]{1,0:T(8,128)(2,1)}, bf16[224,1024]{1,0:T(8,128)(2,1)}, u32[]{:S(2)}, u32[]{:S(2)}) collective-permute-start(bf16[224,1024]{1,0:T(8,128)(2,1)} %pad_maximum_fusion.2.far), channel_id=1, source_target_pairs={{0,1},{1,0},{2,3},{3,2},{4,5},{5,4},{6,7},{7,6},{8,9},{9,8},{10,11... | collective-permute-start | bytes 1376264 | tf_op jit(solution)/shard_map/ppermute | solution.py:35
  107.8 27.2 %collective-permute-start.23 = (bf16[224,1024]{1,0:T(8,128)(2,1)}, bf16[224,1024]{1,0:T(8,128)(2,1)}, u32[]{:S(2)}, u32[]{:S(2)}) collective-permute-start(bf16[224,1024]{1,0:T(8,128)(2,1)} %get-tuple-element.77), channel_id=1, source_target_pairs={{0,2},{2,4},{4,6},{6,8},{8,10},{10,12},{12,14},{14,0},{1,3},{3,5},... | collective-permute-start | bytes 1376264 | tf_op jit(solution)/shard_map/ppermute | solution.py:27
  107.9 27.1 %collective-permute-start.24 = (bf16[224,1024]{1,0:T(8,128)(2,1)}, bf16[224,1024]{1,0:T(8,128)(2,1)}, u32[]{:S(2)}, u32[]{:S(2)}) collective-permute-start(bf16[224,1024]{1,0:T(8,128)(2,1)} %get-tuple-element.78), channel_id=1, source_target_pairs={{0,14},{2,0},{4,2},{6,4},{8,6},{10,8},{12,10},{14,12},{1,15},{3,1}... | collective-permute-start | bytes 1376264 | tf_op jit(solution)/shard_map/ppermute | solution.py:31
  137.3 8.6 %collective-permute-start.1 = (bf16[224,1024]{1,0:T(8,128)(2,1)S(1)}, bf16[224,1024]{1,0:T(8,128)(2,1)}, u32[]{:S(2)}, u32[]{:S(2)}) collective-permute-start(bf16[224,1024]{1,0:T(8,128)(2,1)S(1)} %param.1), channel_id=1, source_target_pairs={{0,32},{16,48},{32,0},{48,16},{64,96},{80,112},{96,64},{112,80},{1... | collective-permute-start | bytes 1376264 | tf_op jit(solution)/shard_map/cond/branch_1_fun/ppermute | solution.py:41
  (32 other events, 448.3 us)
